TPU v7x, 256 devices: a whole 4x4x8 slice. The times are simulated.
256 devices in a mesh: wave: 128 (over z, x, y), deg: 2 (over core).
Axes of the slice: x: 4, y: 4, z: 8, core: 2. Of those that a mesh axis runs over, the one named last changes fastest.
Arguments:
- wind_u: bfloat16 [16, 2, 1280, 5120], P('deg', None, 'wave'), may hold values from -6 to 6
- wind_v: bfloat16 [16, 2, 1280, 5120], P('deg', None, 'wave'), may hold values from -6 to 6
- window_m: int32 [256], replicated, may hold values from 1280 to 2559, as said below
- owner: int32 [256], replicated, may hold values from 0 to 127, as said below
- legendre: bfloat16 [512, 1280, 1280], P('wave', None, 'deg'), may hold values from -12 to 12
Outputs:
- coeffs: float32 [512, 2, 16, 2, 1280], P('wave', None, None, None, 'deg')
- spectra: float32 [2, 16, 1280], P(None, None, ('wave', 'deg'))
Inputs may be any that keep to these rules, and one draw needn't show every extreme that they name: `window_m`: the window's entries name distinct wavenumbers. `owner`: no index appears in more than 4 entries, and some index appears in exactly 4.
All inputs are finite; a program needn't handle non-finite values.
Results may differ from a plain program's by a relative error of at most 0.01.
Values may be sent and summed in bfloat16 or wider, within the bound.
A program may use at most 128 MiB of HBM per device.

v0:
```python
import math

import jax
import jax.numpy as jnp
from jax import lax
from jax.sharding import PartitionSpec as P


def padded(x, sides, width):
    for axis, dim in sides:
        size, length = (lax.axis_size(axis), x.shape[dim])
        up = [(i, (i + 1) % size) for i in range(size - 1)]
        down = [(j, i) for i, j in up]
        last = lax.slice_in_dim(x, length - width, length, axis=dim)
        initial = lax.slice_in_dim(x, 0, width, axis=dim)
        before = lax.ppermute(last, axis, up)
        after = lax.ppermute(initial, axis, down)
        x = jnp.concatenate([before, x, after], axis=dim)
    return x


def slot_numbers(owner, capacity):
    positions = jnp.arange(owner.shape[0], dtype=jnp.int32)
    same_owner = (owner[:, None] == owner[None, :]) & (positions[None, :] < positions[:, None])
    return owner * capacity + jnp.sum(same_owner.astype(jnp.int32), axis=1)


def times_unit(values):
    return jnp.stack([-values[..., 1, :], values[..., 0, :]], axis=-2)


def spectral_terms(flow_u, flow_v, wave_int, degree_int):
    wave_num = wave_int.astype(jnp.float32)
    degree = degree_int.astype(jnp.float32)
    next_degree = degree_int + 1
    eps_here = jnp.sqrt(
        (degree_int * degree_int - wave_int * wave_int).astype(jnp.float32)
        / (4.0 * degree * degree - 1.0)
    )
    eps_next = jnp.sqrt(
        (next_degree * next_degree - wave_int * wave_int).astype(jnp.float32)
        / (4.0 * (degree + 1.0) * (degree + 1.0) - 1.0)
    )
    low_term = (degree + 1.0) * eps_here
    high_term = degree * eps_next
    centre_u = flow_u[..., 1:-1]
    centre_v = flow_v[..., 1:-1]
    vorticity = (
        wave_num * times_unit(centre_v) + low_term * flow_u[..., :-2] - high_term * flow_u[..., 2:]
    )
    divergence = (
        wave_num * times_unit(centre_u) - low_term * flow_v[..., :-2] + high_term * flow_v[..., 2:]
    )
    factor = jnp.expand_dims(lax.rsqrt(degree * (degree + 1.0)), -4)
    return jnp.stack([vorticity, divergence], axis=-4) * factor


def local(wind_u, wind_v, window_m, owner, legendre):
    lev_local, hemispheres, lat_rows, lon_count = wind_u.shape
    entries = window_m.shape[0]
    capacity, half_rows, deg_cols = legendre.shape
    wave_count = lax.axis_size("wave")
    deg_count = lax.axis_size("deg")
    slot_total = capacity * wave_count
    top_degree = 2 * half_rows - 1
    full_cols = deg_cols * deg_count
    lev_total = lev_local * deg_count
    row_width = lev_local * 8
    first_col = lax.axis_index("deg") * deg_cols
    lon_ids = jnp.arange(lon_count, dtype=jnp.int32)
    phases = lon_ids[:, None] * window_m[None, :] % lon_count
    angles = phases.astype(jnp.float32) * (2.0 * math.pi / lon_count)
    dft_table = jnp.concatenate([jnp.cos(angles), -jnp.sin(angles)], axis=1) / lon_count
    table_high = dft_table.astype(jnp.bfloat16)
    table_low = (dft_table - table_high.astype(jnp.float32)).astype(jnp.bfloat16)
    wind_rows = jnp.stack([wind_u, wind_v], axis=1).reshape(-1, lon_count)
    fourier = jnp.dot(wind_rows, table_high, preferred_element_type=jnp.float32) + jnp.dot(
        wind_rows, table_low, preferred_element_type=jnp.float32
    )
    fourier = fourier.reshape(lev_local, 2, hemispheres, lat_rows, 2, entries)
    paired = jnp.stack(
        [fourier[:, :, 0] + fourier[:, :, 1], fourier[:, :, 0] - fourier[:, :, 1]], axis=4
    ).astype(jnp.bfloat16)
    slot_of = slot_numbers(owner, capacity)
    slot_ids = jnp.arange(slot_total, dtype=jnp.int32)
    slot_hits = slot_of[:, None] == slot_ids[None, :]
    placing = slot_hits.astype(jnp.bfloat16)
    by_slot = jnp.einsum(
        "lfjcpe,es->sjlfcp", paired, placing, preferred_element_type=jnp.float32
    ).astype(jnp.bfloat16)
    outgoing = by_slot.reshape(slot_total, lat_rows * row_width)
    slot_base = lax.axis_index("wave") * capacity
    local_hits = lax.dynamic_slice_in_dim(slot_hits.astype(jnp.int32), slot_base, capacity, 1)
    slot_used = jnp.sum(local_hits, axis=0) > 0
    wave_here = jnp.where(slot_used, jnp.sum(local_hits * window_m[:, None], axis=0), half_rows)
    col_ids = first_col + jnp.arange(deg_cols, dtype=jnp.int32)
    live_cols = slot_used[:, None] & (wave_here[:, None] + col_ids[None, :] <= top_degree)
    arrived = lax.all_to_all(outgoing, "wave", split_axis=0, concat_axis=1, tiled=True)
    pieces = lax.all_gather(arrived.reshape(1, capacity, -1), "deg", axis=0, tiled=True)
    groups = pieces.shape[0]
    rows_data = pieces.reshape(groups, capacity, half_rows, row_width)
    main_cols = jnp.einsum(
        "gsjr,sjk->sgrk", rows_data, legendre, preferred_element_type=jnp.float32
    )
    products = main_cols
    products = products.reshape(capacity, lev_total, 2, 2, 2, col_ids.shape[0])
    chosen = jnp.where(col_ids % 2 == 0, products[..., 0, :], products[..., 1, :])
    live_ext = slot_used[:, None] & (wave_here[:, None] + col_ids[None, :] <= top_degree)
    chosen = jnp.where(live_ext[:, None, None, None, :], chosen, 0.0)
    chosen = padded(chosen, (("deg", 4),), 1)
    wave_int = wave_here[:, None, None, None]
    degree_int = (wave_here[:, None] + col_ids[None, :])[:, None, None, :]
    coeffs = spectral_terms(chosen[:, :, 0], chosen[:, :, 1], wave_int, degree_int)
    coeffs = jnp.where(live_cols[:, None, None, None, :], coeffs, 0.0)
    energy = jnp.sum(coeffs * coeffs, axis=3)
    empty_buffer = jnp.zeros((2, lev_total, 2 * full_cols), jnp.float32)
    placed = empty_buffer
    for slot_index in range(capacity):
        offset_col = wave_here[slot_index] - half_rows + first_col
        placed = placed + lax.dynamic_update_slice(
            empty_buffer, energy[slot_index], (0, 0, offset_col)
        )
    spectra = (
        lax.psum_scatter(placed[:, :, :full_cols], ("wave", "deg"), scatter_dimension=2, tiled=True)
        / entries
    )
    return (coeffs, spectra)


def solution(mesh):
    placed = (
        P("deg", None, "wave", None),
        P("deg", None, "wave", None),
        P(),
        P(),
        P("wave", None, "deg"),
    )
    return jax.shard_map(
        local,
        mesh=mesh,
        in_specs=placed,
        out_specs=(P("wave", None, None, None, "deg"), P(None, None, ("wave", "deg"))),
        check_vma=False,
    )
```

profile of v0, /device:TPU:1, one launch (start us, length us, event | category | flops | bytes accessed | tf_op | source)
XLA Modules:
  0.0 469.6 jit_solution(16453297488443842107)
XLA Ops:
  7.2 23.9 %fusion.10 = (f32[5120,256]{1,0:T(8,128)}, f32[5120,256]{1,0:T(8,128)}) fusion(s32[256]{0:T(256)} %param.7), kind=kLoop, calls=%fused_computation.14 | loop fusion | flops 13107200 | bytes 10486784 | tf_op jit(solution)/shard_map/cos | solution.py:73
  31.1 4.6 pad_maximum_fusion
  35.7 3.4 copy.43
  39.1 7.1 %reshape.275 = bf16[320,5120]{1,0:T(8,128)(2,1)} reshape(bf16[8,2,2,10,5120]{4,3,2,1,0:T(8,128)(2,1)} %copy.43) | data formatting | bytes 6553600 | tf_op jit(solution)/shard_map/reshape | solution.py:76
  46.3 7.0 %fusion.3 = f32[320,512]{1,0:T(8,128)S(1)} fusion(bf16[320,5120]{1,0:T(8,128)(2,1)} %reshape.275, f32[5120,256]{1,0:T(8,128)} %get-tuple-element.28, f32[5120,256]{1,0:T(8,128)} %get-tuple-element.27), kind=kOutput, calls=%fused_computation.6 | convolution fusion | flops 1685585920 | bytes 14417920 | tf_op jit(solution)/shard_map/dot_general | solution.py:77
  53.4 4.1 fusion.15
  59.8 46.1 %all_to_all.12 = bf16[128,4,640]{1,0,2:T(8,128)(2,1)} reshape(bf16[512,10,8,2,2,2]{0,5,4,3,2,1:T(2,128)(2,1)S(1)} %copy.47) | data formatting | bytes 1310720 | tf_op jit(solution)/shard_map/all_to_all | solution.py:98
  105.9 20.2 %copy.48 = bf16[128,4,640]{2,1,0:T(4,128)(2,1)} copy(bf16[128,4,640]{1,0,2:T(8,128)(2,1)} %all_to_all.12) | data formatting | bytes 1310720 | tf_op jit(solution)/shard_map/all_to_all | solution.py:98
  126.1 16.3 %all-to-all-start = ((bf16[128,4,640]{2,1,0:T(4,128)(2,1)}), bf16[128,4,640]{2,1,0:T(4,128)(2,1)S(1)}, u32[]{:S(2)}, u32[]{:S(2)}) async-start(bf16[128,4,640]{2,1,0:T(4,128)(2,1)} %copy.48), calls=%async_computation | async-start | bytes 1310720 | tf_op jit(solution)/shard_map/all_to_all | solution.py:98
  142.6 20.8 %all-to-all-done = bf16[128,4,640]{2,1,0:T(4,128)(2,1)S(1)} async-done(((bf16[128,4,640]{2,1,0:T(4,128)(2,1)}), bf16[128,4,640]{2,1,0:T(4,128)(2,1)S(1)}, u32[]{:S(2)}, u32[]{:S(2)}) %all-to-all-start) | async-done | bytes 655392 | tf_op jit(solution)/shard_map/all_to_all | solution.py:98
  166.6 8.7 %all-gather.2.cloned.1.call-done = bf16[2,4,81920]{2,1,0:T(4,128)(2,1)} async-done(((bf16[1,4,81920]{2,1,0:T(4,128)(2,1)}), bf16[2,4,81920]{2,1,0:T(4,128)(2,1)}) %all-gather.2.cloned.1.call-update) | async-done | bytes 1310736 | tf_op jit(solution)/shard_map/all_gather | solution.py:99
  175.3 3.3 reshape.278
  178.6 5.3 %fusion.1 = f32[4,2,64,640]{3,2,1,0:T(8,128)} fusion(bf16[4,1280,640]{2,1,0:T(8,128)(2,1)} %param.9, bf16[2,4,1280,64]{3,2,1,0:T(8,128)(2,1)S(1)} %reshape.278), kind=kOutput, calls=%fused_computation.4 | convolution fusion | flops 838860800 | bytes 9175040 | tf_op jit(solution)/shard_map/gsjr,sjk->sgrk/dot_general | solution.py:102
  183.8 2.1 reshape.279
  185.9 1.0 fusion.68
  187.8 1.3 collective-permute-start
  189.1 3.3 collective-permute-start.1
  193.7 1.0 pad_maximum_fusion.1
  194.8 1.6 slice_negate_fusion
  196.4 1.0 fusion.29
  197.4 1.4 multiply_reduce_fusion
  201.9 1.4 copy.53
  203.3 258.1 %all-reduce.3.cloned.1.call-done = f32[2,16,1280]{1,0,2:T(2,128)} async-done(((f32[2,16,1280]{1,0,2:T(2,128)}), f32[2,16,1280]{1,0,2:T(2,128)}) %all-reduce.3.cloned.1.call-update) | async-done | bytes 163856
  461.5 1.3 dynamic-slice_multiply_fusion
  (53 shorter events, 8.5 us)
Async XLA Ops:
  7.2 23.9 %copy-start.3 = (bf16[8,2,10,5120]{3,1,2,0:T(2,128)(2,1)S(1)}, bf16[8,2,10,5120]{3,1,2,0:T(2,128)(2,1)}, u32[]{:S(2)}) copy-start(bf16[8,2,10,5120]{3,1,2,0:T(2,128)(2,1)} %param.5) | copy-start | bytes 4915204
  7.2 23.9 %copy-start.2 = (bf16[8,2,10,5120]{3,1,2,0:T(2,128)(2,1)S(1)}, bf16[8,2,10,5120]{3,1,2,0:T(2,128)(2,1)}, u32[]{:S(2)}) copy-start(bf16[8,2,10,5120]{3,1,2,0:T(2,128)(2,1)} %param.6) | copy-start | bytes 4915204
  39.1 14.1 %slice-start = ((s8[5242880]{0:T(1024)(128)(4,1)}), s8[1048576]{0:T(1024)(128)(4,1)S(1)}, s32[]{:S(2)}) async-start(s8[5242880]{0:T(1024)(128)(4,1)} %bitcast.67), calls=%async_computation.3 | async-start | bytes 2097152
  46.3 7.0 %slice-start.1 = ((s8[5242880]{0:T(1024)(128)(4,1)}), s8[4194304]{0:T(1024)(128)(4,1)S(1)}, s32[]{:S(2)}) async-start(s8[5242880]{0:T(1024)(128)(4,1)} %bitcast.67), calls=%async_computation.4 | async-start | bytes 8388608
  46.3 7.2 %copy-start = (bf16[320,5120]{1,0:T(8,128)(2,1)S(1)}, bf16[320,5120]{1,0:T(8,128)(2,1)}, u32[]{:S(2)}) copy-start(bf16[320,5120]{1,0:T(8,128)(2,1)} %reshape.275) | copy-start | bytes 9830404
  53.4 4.8 %copy-start.4 = (s32[256]{0:T(256)S(1)}, s32[256]{0:T(256)}, u32[]{:S(2)}) copy-start(s32[256]{0:T(256)} %param.8) | copy-start | bytes 3076
  105.9 58.4 %copy-start.5 = (s32[256]{0:T(256)S(1)}, s32[256]{0:T(256)}, u32[]{:S(2)}) copy-start(s32[256]{0:T(256)} %param.7) | copy-start | bytes 3076
  126.1 37.3 %all-to-all-start = ((bf16[128,4,640]{2,1,0:T(4,128)(2,1)}), bf16[128,4,640]{2,1,0:T(4,128)(2,1)S(1)}, u32[]{:S(2)}, u32[]{:S(2)}) async-start(bf16[128,4,640]{2,1,0:T(4,128)(2,1)} %copy.48), calls=%async_computation | async-start | bytes 1310720 | tf_op jit(solution)/shard_map/all_to_all | solution.py:98
  142.4 32.8 %all-gather.2.cloned.1.call-start = ((), (), s32[]{:S(2)}) async-start(), calls=%async_computation.1 | async-start | bytes 1966080 | tf_op jit(solution)/shard_map/all_gather | solution.py:99
  163.4 0.8 copy-start.1
  164.3 297.2 %all-reduce.3.cloned.1.call-start = ((), (), s32[]{:S(2)}) async-start(), calls=%async_computation.2 | async-start | bytes 2621440
  187.8 5.9 %collective-permute-start = (f32[4,16,2,2,1]{4,3,1,0,2:T(2,128)S(1)}, f32[4,16,2,2,1]{4,3,1,0,2:T(2,128)S(1)}, u32[]{:S(2)}, u32[]{:S(2)}) collective-permute-start(f32[4,16,2,2,1]{4,3,1,0,2:T(2,128)S(1)} %get-tuple-element.12), channel_id=1, source_target_pairs={{0,1},{2,3},{4,5},{6,7},{8,9},{10,11},{12,13},{14,15},{16,17},{18,... | collective-permute-start | bytes 3080 | tf_op jit(solution)/shard_map/ppermute | solution.py:16
  189.1 4.6 collective-permute-start.1
Sparse Core Ops, SparseCore 0:
  164.4 10.8 all-gather.1
  203.4 257.9 all-reduce.2
where the time goes:
time: 471 us; the launch traced here: 470 us
  waiting for transfers between devices  288 us (61%)
  local copies, waits for them, and re-layouts  90.6 us (19%)
  other arithmetic  36.5 us (8%)
  starting transfers between devices  21 us (4%)
  between operations  17 us (4%)
  matrix products  16.9 us (4%)
    unnamed x3, waiting for transfers between devices  258 us
    all_to_all x2, local copies, waits for them, and re-layouts, local(): lax.all_to_all(outgoing, 'wave', split_axis=0, concat_axis=1, tiled=True)  66.3 us
    cos x1, other arithmetic, local(): jnp.cos(angles)  23.9 us
    all_to_all x1, waiting for transfers between devices, local(): lax.all_to_all(outgoing, 'wave', split_axis=0, concat_axis=1, tiled=True)  20.8 us
    all_to_all x1, starting transfers between devices, local(): lax.all_to_all(outgoing, 'wave', split_axis=0, concat_axis=1, tiled=True)  16.3 us
  transfers between devices with their start and end apart: 5, of which 3 were waited for; matrix products, arithmetic and copies ran while one was open for 0% of the time, Pallas kernels for 0%

commit v1 on v0

v1 whole, which is shorter than its diff:
```python
import functools
import math

import jax
import jax.numpy as jnp
import numpy as np
from jax import lax
from jax.experimental import pallas as pl
from jax.experimental.pallas import tpu as pltpu
from jax.sharding import PartitionSpec as P

MESH = pl.DeviceIdType.MESH
BF16 = jnp.bfloat16
F32 = jnp.float32
VMEM_BYTES = 56 * 1024 * 1024

NLON = 5120
LANES = 128
COARSE = NLON // LANES
ENTRIES = 256
ROWS = 10
HALF = 1280
COLS = 640
CHUNK = 4

NT = (((1,), (1,)), ((), ()))


def row_order():
    source = np.arange(640).reshape(2, 2, 2, 8, ROWS)
    wanted = source.transpose(4, 1, 2, 3, 0).reshape(-1)
    return np.eye(640, dtype=np.float32)[wanted].astype(jnp.bfloat16)


def group_order():
    source = np.arange(160).reshape(ROWS, 16)
    wanted = source.transpose(1, 0).reshape(-1)
    return np.eye(160, dtype=np.float32)[wanted].astype(jnp.bfloat16)


def unit_waves(steps, window, period):
    phase = steps * window
    phase = phase - period * jnp.round(phase * (1.0 / period))
    angle = phase * (2.0 * math.pi / period)
    return jnp.cos(angle), jnp.sin(angle)


def dft_kernel(
    wind_u, wind_v, window_ref, slot_ref, order_ref, group_ref, out_ref,
    winds, coarse_cos, coarse_sin, fine_cos, fine_sin, total, split, sems,
):
    for chunk in range(COARSE // CHUNK):
        for inner in range(CHUNK):
            tile = chunk * CHUNK + inner
            for which, ref in enumerate((wind_u, wind_v)):
                pltpu.make_async_copy(ref.at[:, tile], winds.at[tile, which], sems.at[chunk]).start()
    window = window_ref[...].astype(F32)
    coarse_steps = lax.broadcasted_iota(jnp.int32, (COARSE, ENTRIES), 0).astype(F32)
    fine_steps = lax.broadcasted_iota(jnp.int32, (LANES, ENTRIES), 0).astype(F32)
    cos_part, sin_part = unit_waves(coarse_steps, window, float(COARSE))
    coarse_cos[...] = cos_part
    coarse_sin[...] = sin_part
    cos_part, sin_part = unit_waves(fine_steps, window, float(NLON))
    fine_cos[...] = cos_part * (1.0 / NLON)
    fine_sin[...] = sin_part * (1.0 / NLON)
    total[...] = jnp.zeros_like(total)

    def step(chunk, carry):
        part = winds.at[pl.ds(chunk * CHUNK, CHUNK)]
        pltpu.make_async_copy(part, part, sems.at[chunk]).wait()
        cos_b = fine_cos[...]
        sin_b = fine_sin[...]
        highs, lows, pieces = [], [], []
        for inner in range(CHUNK):
            tile = chunk * CHUNK + inner
            cos_a = coarse_cos[pl.ds(tile, 1), :]
            sin_a = coarse_sin[pl.ds(tile, 1), :]
            table = jnp.concatenate(
                [cos_a * cos_b - sin_a * sin_b, -(sin_a * cos_b + cos_a * sin_b)], axis=1
            )
            high = table.astype(BF16)
            highs.append(high)
            lows.append((table - high.astype(F32)).astype(BF16))
            pieces.append(winds.at[tile].reshape(320, LANES)[...])
        data = jnp.concatenate(pieces, axis=1)
        total[...] += jnp.dot(
            data, jnp.concatenate(highs, axis=0), preferred_element_type=F32
        ) + jnp.dot(data, jnp.concatenate(lows, axis=0), preferred_element_type=F32)
        return carry

    lax.fori_loop(0, COARSE // CHUNK, step, 0)
    for tile in range(4):
        split[tile] = total[:, LANES * tile : LANES * tile + LANES]

    def hemisphere(h):
        return jnp.concatenate([split[tile, pl.ds(h, 160, stride=2), :] for tile in range(4)], axis=1)

    north = hemisphere(0)
    south = hemisphere(1)
    even = (north + south).astype(BF16)
    odd = (north - south).astype(BF16)
    paired = jnp.concatenate(
        [even[:, :ENTRIES], odd[:, :ENTRIES], even[:, ENTRIES:], odd[:, ENTRIES:]], axis=0
    )
    ordered = jnp.dot(order_ref[...], paired, preferred_element_type=F32).astype(BF16)
    empty = jnp.zeros((64, ENTRIES), BF16)
    blocks = []
    for row in range(ROWS):
        block = ordered[64 * row : 64 * row + 64]
        blocks.append(jnp.concatenate([block, empty], axis=1))
        blocks.append(jnp.concatenate([empty, block], axis=1))
    blocks = jnp.concatenate(blocks, axis=0)
    pair_ids = 2 * lax.broadcasted_iota(jnp.int32, (256, ENTRIES), 0)
    slots = slot_ref[...]
    placing = jnp.concatenate(
        [
            (slots == pair_ids).astype(F32).astype(BF16),
            (slots == pair_ids + 1).astype(F32).astype(BF16),
        ],
        axis=1,
    )
    placed = lax.dot_general(placing, blocks, NT, preferred_element_type=F32).astype(BF16)
    stacked = jnp.concatenate(
        [
            jnp.concatenate(
                [placed[16 * g : 16 * g + 16, LANES * row : LANES * row + LANES] for g in range(16)],
                axis=1,
            )
            for row in range(ROWS)
        ],
        axis=0,
    )
    result = jnp.dot(group_ref[...], stacked, preferred_element_type=F32).astype(BF16)
    for g in range(16):
        out_ref[160 * g : 160 * g + 160, :] = result[:, LANES * g : LANES * g + LANES]


def dft_call(wind_u, wind_v, window_m, slot_of):
    vmem = pl.BlockSpec(memory_space=pltpu.VMEM)
    hbm = pl.BlockSpec(memory_space=pl.ANY)

    def tiles(wind):
        split = wind.transpose(0, 2, 1, 3).reshape(8, ROWS, 2, COARSE, LANES)
        return split.transpose(0, 1, 3, 2, 4).reshape(80, COARSE, 2, LANES)

    return pl.pallas_call(
        dft_kernel,
        out_shape=jax.ShapeDtypeStruct((2560, LANES), BF16),
        in_specs=[hbm, hbm, vmem, vmem, vmem, vmem],
        out_specs=vmem,
        scratch_shapes=[
            pltpu.VMEM((COARSE, 2, 80, 2, LANES), BF16),
            pltpu.VMEM((COARSE, ENTRIES), F32),
            pltpu.VMEM((COARSE, ENTRIES), F32),
            pltpu.VMEM((LANES, ENTRIES), F32),
            pltpu.VMEM((LANES, ENTRIES), F32),
            pltpu.VMEM((320, 2 * ENTRIES), F32),
            pltpu.VMEM((4, 320, LANES), F32),
            pltpu.SemaphoreType.DMA((COARSE // CHUNK,)),
        ],
        compiler_params=pltpu.CompilerParams(vmem_limit_bytes=VMEM_BYTES),
    )(
        tiles(wind_u), tiles(wind_v), window_m[None, :], slot_of[None, :],
        jnp.asarray(row_order()), jnp.asarray(group_order()),
    )


def exchange_kernel(
    send_ref, table_ref, data_ref, edge_ref,
    send_sem, recv_sem, core_send, core_recv, edge_send, edge_recv,
):
    me = lax.axis_index("wave")
    core = lax.axis_index("deg")
    other = 1 - core
    plane = me // 16
    inside = me % 16

    def partner(step):
        return (plane + step // 16) % 8 * 16 + (inside // 4 + step // 4) % 4 * 4 + (inside + step) % 4

    barrier = pltpu.get_barrier_semaphore()

    def greet(step, carry):
        pl.semaphore_signal(barrier, inc=1, device_id=(partner(step), core), device_id_type=MESH)
        return carry

    lax.fori_loop(1, 128, greet, 0)
    pl.semaphore_signal(barrier, inc=1, device_id=(me, other), device_id_type=MESH)
    pl.semaphore_wait(barrier, 128)

    edge = pltpu.make_async_remote_copy(
        src_ref=table_ref.at[:, :, pl.ds(pl.multiple_of(other * 512, LANES), LANES)],
        dst_ref=edge_ref, send_sem=edge_send, recv_sem=edge_recv,
        device_id=(me, other), device_id_type=MESH,
    )
    own = pltpu.make_async_copy(send_ref.at[me], data_ref.at[core, :, me], recv_sem.at[0])
    own.start()

    def send(step, carry):
        target = partner(step)
        pltpu.make_async_remote_copy(
            src_ref=send_ref.at[target], dst_ref=data_ref.at[core, :, me],
            send_sem=send_sem, recv_sem=recv_sem.at[step // 16],
            device_id=(target, core), device_id_type=MESH,
        ).start()
        return carry

    lax.fori_loop(1, 128, send, 0)
    edge.start()

    def forward(step):
        group = (plane + 8 - step) % 8
        part = data_ref.at[core, :, pl.ds(group * 16, 16)]
        return part, pltpu.make_async_remote_copy(
            src_ref=part, dst_ref=part, send_sem=core_send.at[step], recv_sem=core_recv.at[step],
            device_id=(me, other), device_id_type=MESH,
        )

    for step in range(8):
        part, copy = forward(step)
        pltpu.make_async_copy(part, part, recv_sem.at[step]).wait()
        copy.start()
    for step in range(8):
        part, copy = forward(step)
        copy.wait_send()
        group = (plane + 8 - step) % 8
        arrived = data_ref.at[other, :, pl.ds(group * 16, 16)]
        pltpu.make_async_copy(arrived, arrived, core_recv.at[step]).wait()
    edge.wait()
    sent = send_ref.at[pl.ds(0, 127)]
    pltpu.make_async_copy(sent, sent, send_sem).wait()


def exchange_call(outgoing, legendre):
    hbm = pl.BlockSpec(memory_space=pl.ANY)
    dma = pltpu.SemaphoreType.DMA
    return pl.pallas_call(
        exchange_kernel,
        out_shape=(
            jax.ShapeDtypeStruct((2, 2, 128, 5, 2, LANES), BF16),
            jax.ShapeDtypeStruct((4, HALF, LANES), BF16),
        ),
        in_specs=[hbm, hbm],
        out_specs=(hbm, hbm),
        scratch_shapes=[dma, dma((8,)), dma((8,)), dma((8,)), dma, dma],
        compiler_params=pltpu.CompilerParams(
            collective_id=0, has_side_effects=True, vmem_limit_bytes=VMEM_BYTES
        ),
    )(outgoing.reshape(128, 2, 5, 2, LANES), legendre)


def project_kernel(meta, data_ref, table_ref, edge_ref, out_ref, energy_ref, summed, split):
    slot = pl.program_id(0)
    core = meta[8]
    wave_int = meta[slot]
    used = meta[4 + slot]
    half = slot % 2
    row_ids = lax.broadcasted_iota(jnp.int32, (64, LANES), 0)
    col_ids = lax.broadcasted_iota(jnp.int32, (64, LANES), 1)
    picking = (col_ids == row_ids + 64 * half).astype(F32).astype(BF16)
    rows = jnp.concatenate(
        [
            lax.dot_general(picking, data_ref[h, 0], NT, preferred_element_type=F32).astype(BF16)
            for h in range(2)
        ],
        axis=0,
    )
    main = jnp.dot(rows, table_ref[0], preferred_element_type=F32)
    beside = jnp.dot(rows, edge_ref[0], preferred_element_type=F32)

    def field(values, parity, f):
        return jnp.concatenate(
            [values[64 * h + 32 * parity + 16 * f : 64 * h + 32 * parity + 16 * f + 16] for h in range(2)],
            axis=0,
        )

    shape = (32, COLS)
    col = lax.broadcasted_iota(jnp.int32, shape, 1)
    degree_int = wave_int + core * COLS + col
    last = jnp.where(used > 0, 2 * HALF - 1, -1)
    live = degree_int <= last
    even_col = col % 2 == 0
    edge_live = wave_int + COLS - core <= last
    flows, before, after = [], [], []
    for f in range(2):
        flow = jnp.where(even_col, field(main, 0, f), field(main, 1, f))
        flow = jnp.where(live, flow, 0.0)
        border = jnp.where(core == 0, field(beside, 0, f)[:, :1], field(beside, 1, f)[:, LANES - 1 :])
        border = jnp.where(edge_live, border, 0.0)
        first = jnp.where(core == 1, border, 0.0)
        final = jnp.where(core == 0, border, 0.0)
        flows.append(flow)
        before.append(jnp.where(col == 0, first, pltpu.roll(flow, 1, 1)))
        after.append(jnp.where(col == COLS - 1, final, pltpu.roll(flow, COLS - 1, 1)))

    line = lax.broadcasted_iota(jnp.int32, (8, COLS), 1)
    degree_row = wave_int + core * COLS + line
    degree = degree_row.astype(F32)
    next_row = degree_row + 1
    squared = wave_int * wave_int
    eps_here = jnp.sqrt((degree_row * degree_row - squared).astype(F32) / (4.0 * degree * degree - 1.0))
    eps_next = jnp.sqrt(
        (next_row * next_row - squared).astype(F32) / (4.0 * (degree + 1.0) * (degree + 1.0) - 1.0)
    )
    factor = lax.rsqrt(degree * (degree + 1.0))
    low_term = ((degree + 1.0) * eps_here * factor)[:1]
    high_term = (degree * eps_next * factor)[:1]
    wave_term = (wave_int.astype(F32) * factor)[:1]
    is_real = lax.broadcasted_iota(jnp.int32, shape, 0) % 2 == 0

    def times_unit(values):
        return jnp.where(is_real, -pltpu.roll(values, 31, 0), pltpu.roll(values, 1, 0))

    vorticity = wave_term * times_unit(flows[1]) + low_term * before[0] - high_term * after[0]
    divergence = wave_term * times_unit(flows[0]) - low_term * before[1] + high_term * after[1]
    offset = wave_int - HALF + core * COLS

    @pl.when(slot == 0)
    def _():
        summed[...] = jnp.zeros_like(summed)

    for q, values in enumerate((vorticity, divergence)):
        values = jnp.where(live, values, 0.0)
        out_ref[0, q] = values.reshape(16, 2, COLS)
        wide = jnp.concatenate([values * values, jnp.zeros(shape, F32)], axis=1)
        summed[32 * q : 32 * q + 32, :] += pltpu.roll(wide, offset, 1)

    @pl.when(slot == 3)
    def _():
        for tile in range(HALF // LANES):
            split[tile] = summed[:, LANES * tile : LANES * tile + LANES]
        energy_ref[...] = jnp.concatenate(
            [
                split[tile, pl.ds(0, 32, stride=2), :] + split[tile, pl.ds(1, 32, stride=2), :]
                for tile in range(HALF // LANES)
            ],
            axis=1,
        )


def project_call(meta, data, legendre, edge):
    return pl.pallas_call(
        project_kernel,
        grid=(4,),
        out_shape=(
            jax.ShapeDtypeStruct((4, 2, 16, 2, COLS), F32),
            jax.ShapeDtypeStruct((32, HALF), F32),
        ),
        in_specs=[
            pl.BlockSpec(memory_space=pltpu.SMEM),
            pl.BlockSpec((2, 1, HALF, LANES), lambda s: (0, s // 2, 0, 0)),
            pl.BlockSpec((1, HALF, COLS), lambda s: (s, 0, 0)),
            pl.BlockSpec((1, HALF, LANES), lambda s: (s, 0, 0)),
        ],
        out_specs=(
            pl.BlockSpec((1, 2, 16, 2, COLS), lambda s: (s, 0, 0, 0, 0)),
            pl.BlockSpec((32, HALF), lambda s: (0, 0)),
        ),
        scratch_shapes=[
            pltpu.VMEM((64, HALF), F32),
            pltpu.VMEM((HALF // LANES, 64, LANES), F32),
        ],
        compiler_params=pltpu.CompilerParams(vmem_limit_bytes=VMEM_BYTES),
    )(meta, data, legendre, edge)


def reduce_kernel(energy_ref, out_ref, send_a, recv_a, send_b, recv_b, send_sems, recv_sems):
    me = lax.axis_index("wave")
    core = lax.axis_index("deg")
    plane = me // 16
    inside = me % 16

    def plane_partner(step):
        return (plane + step // 2) % 8, (core + step) % 2

    def inside_partner(step):
        return (inside + step // 2) % 16, (core + step) % 2

    barrier = pltpu.get_barrier_semaphore()

    def greet_planes(step, carry):
        there, side = plane_partner(step)
        pl.semaphore_signal(barrier, inc=1, device_id=(there * 16 + inside, side), device_id_type=MESH)
        return carry

    def greet_inside(step, carry):
        there, side = inside_partner(step)
        pl.semaphore_signal(barrier, inc=1, device_id=(plane * 16 + there, side), device_id_type=MESH)
        return carry

    lax.fori_loop(1, 16, greet_planes, 0)
    lax.fori_loop(2, 32, greet_inside, 0)
    lane = lax.broadcasted_iota(jnp.int32, (8, 3 * LANES), 1)
    for there in range(8):
        for q in range(2):
            upper = energy_ref[16 * q : 16 * q + 8, :]
            lower = energy_ref[16 * q + 8 : 16 * q + 16, :]
            upper = pltpu.roll(upper, (HALF - 160 * there) % HALF, 1)[:, : 3 * LANES]
            lower = pltpu.roll(lower, (HALF + 160 - 160 * there) % HALF, 1)[:, : 3 * LANES]
            send_a[2 * there + q] = jnp.where(lane < 160, upper, lower)
    recv_a[2 * plane + core] = send_a[2 * plane + core]
    pl.semaphore_wait(barrier, 45)

    def send_planes(step, carry):
        there, side = plane_partner(step)
        pltpu.make_async_remote_copy(
            src_ref=send_a.at[2 * there + side], dst_ref=recv_a.at[2 * plane + core],
            send_sem=send_sems.at[0], recv_sem=recv_sems.at[0],
            device_id=(there * 16 + inside, side), device_id_type=MESH,
        ).start()
        return carry

    lax.fori_loop(1, 16, send_planes, 0)
    arrived = recv_a.at[pl.ds(0, 15)]
    pltpu.make_async_copy(arrived, arrived, recv_sems.at[0]).wait()
    chunk = recv_a[0]
    for index in range(1, 16):
        chunk = chunk + recv_a[index]
    narrow = lane[:, :LANES]
    for there in range(32):
        upper = pltpu.roll(chunk, (384 - 5 * there) % 384, 1)[:, :LANES]
        lower = pltpu.roll(chunk, 384 - 96 - 5 * there, 1)[:, :LANES]
        send_b[there] = jnp.where(narrow < 64, upper, lower)
    recv_b[2 * inside + core] = send_b[2 * inside + core]

    def send_inside(step, carry):
        there, side = inside_partner(step)
        pltpu.make_async_remote_copy(
            src_ref=send_b.at[2 * there + side], dst_ref=recv_b.at[2 * inside + core],
            send_sem=send_sems.at[1], recv_sem=recv_sems.at[1],
            device_id=(plane * 16 + there, side), device_id_type=MESH,
        ).start()
        return carry

    lax.fori_loop(1, 32, send_inside, 0)
    arrived = recv_b.at[pl.ds(0, 31)]
    pltpu.make_async_copy(arrived, arrived, recv_sems.at[1]).wait()
    for q in range(2):
        chunk = recv_b[q]
        for index in range(1, 16):
            chunk = chunk + recv_b[2 * index + q]
        turned = jnp.transpose(chunk * (1.0 / ENTRIES), (1, 0))
        out_ref[:, q, :] = jnp.concatenate([turned[:5], turned[64:69]], axis=1)
    sent = send_a.at[pl.ds(0, 15)]
    pltpu.make_async_copy(sent, sent, send_sems.at[0]).wait()
    sent = send_b.at[pl.ds(0, 31)]
    pltpu.make_async_copy(sent, sent, send_sems.at[1]).wait()


def reduce_call(energy):
    vmem = pl.BlockSpec(memory_space=pltpu.VMEM)
    return pl.pallas_call(
        reduce_kernel,
        out_shape=jax.ShapeDtypeStruct((5, 2, 16), F32),
        in_specs=[vmem],
        out_specs=vmem,
        scratch_shapes=[
            pltpu.VMEM((16, 8, 3 * LANES), F32),
            pltpu.VMEM((16, 8, 3 * LANES), F32),
            pltpu.VMEM((32, 8, LANES), F32),
            pltpu.VMEM((32, 8, LANES), F32),
            pltpu.SemaphoreType.DMA((2,)),
            pltpu.SemaphoreType.DMA((2,)),
        ],
        compiler_params=pltpu.CompilerParams(collective_id=1, has_side_effects=True),
    )(energy)


def slot_numbers(owner):
    positions = jnp.arange(owner.shape[0], dtype=jnp.int32)
    same_owner = (owner[:, None] == owner[None, :]) & (positions[:, None] < positions[None, :])
    return owner * 4 + jnp.sum(same_owner.astype(jnp.int32), axis=0)


def local(wind_u, wind_v, window_m, owner, legendre):
    slot_of = slot_numbers(owner)
    here = lax.axis_index("wave") * 4 + jnp.arange(4, dtype=jnp.int32)
    hits = (slot_of[None, :] == here[:, None]).astype(jnp.int32)
    used = jnp.sum(hits, axis=1)
    wave_here = jnp.where(used > 0, jnp.sum(hits * window_m[None, :], axis=1), HALF)
    core = lax.axis_index("deg").astype(jnp.int32)
    meta = jnp.concatenate([wave_here, used, core[None]])
    outgoing = dft_call(wind_u, wind_v, window_m, slot_of)
    data, edge = exchange_call(outgoing, legendre)
    coeffs, energy = project_call(meta, data.reshape(2, 2, HALF, LANES), legendre, edge)
    spectra = reduce_call(energy).transpose(1, 2, 0)
    return (coeffs, spectra)


def solution(mesh):
    placed = (
        P("deg", None, "wave", None),
        P("deg", None, "wave", None),
        P(),
        P(),
        P("wave", None, "deg"),
    )
    return jax.shard_map(
        local,
        mesh=mesh,
        in_specs=placed,
        out_specs=(P("wave", None, None, None, "deg"), P(None, None, ("wave", "deg"))),
        check_vma=False,
    )
```

time: 471 us -> 78.8 us (0.17)
  waiting for transfers between devices: 288 us -> 0 us
  local copies, waits for them, and re-layouts: 90.6 us -> 1.29 us
  Pallas kernels: 0 us -> 73.5 us
  other arithmetic: 36.5 us -> 3.13 us
  starting transfers between devices: 21 us -> 0 us
  matrix products: 16.9 us -> 0 us
  between operations: 17 us -> 0.67 us
    unnamed x3 -> x0, waiting for transfers between devices: 258 us -> none
    pallas_call x0 -> x4, Pallas kernels: none -> 73.5 us  [the longest x1 36.4 us: exchange_call(): pl.pallas_call(exchange_kernel, out_shape=(jax.ShapeDtypeStruct((2, 2, 12...]
    all_to_all x2 -> x0, local copies, waits for them, and re-layouts: 66.3 us -> none  [local(): lax.all_to_all(outgoing, 'wave', split_axis=0, concat_axis=1, tiled=True)]
    cos x1 -> x0, other arithmetic: 23.9 us -> none  [local(): jnp.cos(angles)]
    all_to_all x1 -> x0, waiting for transfers between devices: 20.8 us -> none  [local(): lax.all_to_all(outgoing, 'wave', split_axis=0, concat_axis=1, tiled=True)]
    dot_general x4 -> x0, matrix products: 16.9 us -> none  [the longest x1 6.97 us: local(): jnp.dot(wind_rows, table_high, preferred_element_type=jnp.float32)]
    all_to_all x1 -> x0, starting transfers between devices: 16.3 us -> none  [local(): lax.all_to_all(outgoing, 'wave', split_axis=0, concat_axis=1, tiled=True)]
    reshape x4 -> x0, local copies, waits for them, and re-layouts: 12.9 us -> none  [the longest x1 7.14 us: local(): wind_rows = jnp.stack([wind_u, wind_v], axis=1).reshape(-1, lon_count)]
  transfers between devices with their start and end apart: 5 -> 0, of which waited for: 3 -> 0; matrix products, arithmetic and copies ran while one was open for 0% -> 0% of each run, Pallas kernels for 0% -> 0%
where the time goes in v1:
time: 78.8 us; the launch traced here: 78.6 us
  Pallas kernels  73.5 us (93%)
  other arithmetic  3.13 us (4%)
  local copies, waits for them, and re-layouts  1.29 us (2%)
    pallas_call x1, Pallas kernels, exchange_call(): pl.pallas_call(exchange_kernel, out_shape=(jax.ShapeDtypeStruct((2, 2, 12...  36.4 us
    pallas_call x1, Pallas kernels, reduce_call(): pl.pallas_call(reduce_kernel, out_shape=jax.ShapeDtypeStruct((5, 2, 16),...  18 us
    pallas_call x1, Pallas kernels, dft_call(): pl.pallas_call(dft_kernel, out_shape=jax.ShapeDtypeStruct((2560, LANES),...  11.7 us
    pallas_call x1, Pallas kernels, project_call(): pl.pallas_call(project_kernel, grid=(4,), out_shape=(jax.ShapeDtypeStruct...  7.39 us

profile of v1, /device:TPU:1, one launch (start us, length us, event | category | flops | bytes accessed | tf_op | source)
XLA Modules:
  0.0 78.6 jit_solution(10467843869488749213)
XLA Ops:
  0.6 0.9 %convert_reduce_fusion = s32[256]{0:T(256)S(1)} fusion(s32[256]{0:T(256)} %param.10), kind=kLoop, calls=%fused_computation | loop fusion | flops 327424 | bytes 2048 | tf_op jit(solution)/shard_map/reduce_sum | solution.py:472
  1.5 0.7 multiply_add_fusion
  2.2 0.0 copy-start
  2.2 0.9 %fusion.2 = (s32[4]{0:T(128)S(1)}, s32[4]{0:T(128)S(1)}) fusion(s32[256]{0:T(256)} %param.9, s32[256]{0:T(256)S(1)} %multiply_add_fusion, s32[4]{0:T(128)S(1)} %iota_add_fusion), kind=kLoop, calls=%fused_computation.6 | loop fusion | flops 5112 | bytes 2096 | tf_op jit(solution)/shard_map/reduce_sum | solution.py:480
  3.1 0.7 pad_add_fusion.meta
  3.8 0.0 copy-done
  3.8 11.7 %shard_map.86 = bf16[2560,128]{1,0:T(8,128)(2,1)} custom-call(bf16[80,40,2,128]{3,2,1,0:T(2,128)(2,1)} %bitcast.21, bf16[80,40,2,128]{3,2,1,0:T(2,128)(2,1)} %bitcast.22, s32[1,256]{1,0:T(1,128)} %bitcast.26, s32[1,256]{1,0:T(1,128)} %bitcast.25, bf16[640,640]{1,0:T(8,128)(2,1)} %constant.21.clone.order_ref, bf16[160,160]{1,0:T(8,128)(2,1)} %constant.22.clone.group_ref), custom_call_target="tpu_custom_call" | custom-call | tf_op jit(solution)/shard_map/pallas_call | solution.py:146
  15.5 36.4 %shard_map.87 = (bf16[2,2,128,5,2,128]{5,4,3,2,1,0:T(2,128)(2,1)}, bf16[4,1280,128]{2,1,0:T(8,128)(2,1)}) custom-call(bf16[128,2,5,2,128]{4,3,2,1,0:T(2,128)(2,1)} %bitcast.20, bf16[4,1280,640]{2,1,0:T(8,128)(2,1)} %table_ref.3), custom_call_target="tpu_custom_call" | custom-call | tf_op jit(solution)/shard_map/pallas_call | solution.py:237
  51.9 7.4 %shard_map.88 = (f32[4,2,16,2,640]{4,3,2,1,0:T(2,128)}, f32[32,1280]{1,0:T(8,128)}) custom-call(s32[9]{0:T(128)} %pad_add_fusion.meta, bf16[2,2,1280,128]{3,2,1,0:T(8,128)(2,1)} %bitcast.23, bf16[4,1280,640]{2,1,0:T(8,128)(2,1)} %table_ref.3, bf16[4,1280,128]{2,1,0:T(8,128)(2,1)} %get-tuple-element.7.edge_ref), custom_call_target="tpu_custom_call" | custom-call | tf_op jit(solution)/shard_map/pallas_call | solution.py:342
  59.3 18.0 %shard_map.89 = f32[5,2,16]{2,1,0:T(2,128)} custom-call(f32[32,1280]{1,0:T(8,128)} %get-tuple-element.9.energy_ref), custom_call_target="tpu_custom_call" | custom-call | tf_op jit(solution)/shard_map/pallas_call | solution.py:452
  77.3 1.3 %copy.14 = f32[2,16,5]{1,0,2:T(2,128)} copy(f32[2,16,5]{1,0,2:T(2,128)} %bitcast.24) | data formatting | bytes 1280
  (2 shorter events, 0.0 us)
Async XLA Ops:
  2.2 1.6 %copy-start = (s32[256]{0:T(256)}, s32[256]{0:T(256)S(1)}, u32[]{:S(2)}) copy-start(s32[256]{0:T(256)S(1)} %multiply_add_fusion) | copy-start | bytes 3076

commit v2 on v1

--- a/solution.py
+++ b/solution.py
@@ -167,7 +167,7 @@
 
 def exchange_kernel(
     send_ref, table_ref, data_ref, edge_ref,
-    send_sem, recv_sem, core_send, core_recv, edge_send, edge_recv,
+    send_sem, recv_sem, core_send, core_recv, edge_send, edge_recv, meet_x, meet_y,
 ):
     me = lax.axis_index("wave")
     core = lax.axis_index("deg")
@@ -175,56 +175,75 @@
     plane = me // 16
     inside = me % 16
 
+    row = inside // 4
+    column = inside % 4
+
     def partner(step):
-        return (plane + step // 16) % 8 * 16 + (inside // 4 + step // 4) % 4 * 4 + (inside + step) % 4
+        turn = step % 8
+        away = (4 + (turn + 1) // 2 * (1 - 2 * (turn % 2)) + 8) % 8
+        return (plane + away) % 8 * 16 + (row + step // 32) % 4 * 4 + (column + step // 8) % 4
+
+    def along_z(step):
+        return (plane + step) % 8 * 16 + inside
+
+    def along_x(step):
+        return plane * 16 + (row + step) % 4 * 4 + column
+
+    def along_y(step):
+        return plane * 16 + row * 4 + (column + step) % 4
+
+    def greet(sem, where, count):
+        for step in range(1, count):
+            pl.semaphore_signal(sem, inc=1, device_id=(where(step), core), device_id_type=MESH)
 
     barrier = pltpu.get_barrier_semaphore()
-
-    def greet(step, carry):
-        pl.semaphore_signal(barrier, inc=1, device_id=(partner(step), core), device_id_type=MESH)
-        return carry
-
-    lax.fori_loop(1, 128, greet, 0)
+    greet(barrier, along_z, 8)
+    greet(barrier, along_x, 4)
+    greet(barrier, along_y, 4)
     pl.semaphore_signal(barrier, inc=1, device_id=(me, other), device_id_type=MESH)
-    pl.semaphore_wait(barrier, 128)
+    pl.semaphore_wait(barrier, 14)
+    greet(meet_x, along_x, 4)
+    pl.semaphore_wait(meet_x, 3)
+    greet(meet_y, along_y, 4)
+    pl.semaphore_wait(meet_y, 3)
 
     edge = pltpu.make_async_remote_copy(
         src_ref=table_ref.at[:, :, pl.ds(pl.multiple_of(other * 512, LANES), LANES)],
         dst_ref=edge_ref, send_sem=edge_send, recv_sem=edge_recv,
         device_id=(me, other), device_id_type=MESH,
     )
-    own = pltpu.make_async_copy(send_ref.at[me], data_ref.at[core, :, me], recv_sem.at[0])
+    own = pltpu.make_async_copy(send_ref.at[me], data_ref.at[core, :, plane, inside], recv_sem.at[0])
     own.start()
 
     def send(step, carry):
         target = partner(step)
         pltpu.make_async_remote_copy(
-            src_ref=send_ref.at[target], dst_ref=data_ref.at[core, :, me],
-            send_sem=send_sem, recv_sem=recv_sem.at[step // 16],
+            src_ref=send_ref.at[target], dst_ref=data_ref.at[core, :, plane, inside],
+            send_sem=send_sem, recv_sem=recv_sem.at[step // 8],
             device_id=(target, core), device_id_type=MESH,
         ).start()
         return carry
 
-    lax.fori_loop(1, 128, send, 0)
+    lax.fori_loop(0, 7, send, 0)
+    lax.fori_loop(8, 128, send, 0)
     edge.start()
 
     def forward(step):
-        group = (plane + 8 - step) % 8
-        part = data_ref.at[core, :, pl.ds(group * 16, 16)]
-        return part, pltpu.make_async_remote_copy(
+        source = (row + 4 - step // 4) % 4 * 4 + (column + 16 - step) % 4
+        part = data_ref.at[core, :, :, source]
+        return source, part, pltpu.make_async_remote_copy(
             src_ref=part, dst_ref=part, send_sem=core_send.at[step], recv_sem=core_recv.at[step],
             device_id=(me, other), device_id_type=MESH,
         )
 
-    for step in range(8):
-        part, copy = forward(step)
+    for step in range(16):
+        source, part, copy = forward(step)
         pltpu.make_async_copy(part, part, recv_sem.at[step]).wait()
         copy.start()
-    for step in range(8):
-        part, copy = forward(step)
+    for step in range(16):
+        source, part, copy = forward(step)
         copy.wait_send()
-        group = (plane + 8 - step) % 8
-        arrived = data_ref.at[other, :, pl.ds(group * 16, 16)]
+        arrived = data_ref.at[other, :, :, source]
         pltpu.make_async_copy(arrived, arrived, core_recv.at[step]).wait()
     edge.wait()
     sent = send_ref.at[pl.ds(0, 127)]
@@ -237,12 +256,15 @@
     return pl.pallas_call(
         exchange_kernel,
         out_shape=(
-            jax.ShapeDtypeStruct((2, 2, 128, 5, 2, LANES), BF16),
+            jax.ShapeDtypeStruct((2, 2, 8, 16, 5, 2, LANES), BF16),
             jax.ShapeDtypeStruct((4, HALF, LANES), BF16),
         ),
         in_specs=[hbm, hbm],
         out_specs=(hbm, hbm),
-        scratch_shapes=[dma, dma((8,)), dma((8,)), dma((8,)), dma, dma],
+        scratch_shapes=[
+            dma, dma((16,)), dma((16,)), dma((16,)), dma, dma,
+            pltpu.SemaphoreType.REGULAR, pltpu.SemaphoreType.REGULAR,
+        ],
         compiler_params=pltpu.CompilerParams(
             collective_id=0, has_side_effects=True, vmem_limit_bytes=VMEM_BYTES
         ),

time: 78.8 us -> 76.6 us (0.972)
  Pallas kernels: 73.5 us -> 71.3 us
    pallas_call x1, Pallas kernels: 36.4 us -> 32.7 us  [exchange_call(): pl.pallas_call(exchange_kernel, out_shape=(jax.ShapeDtypeStruct((2, 2, 8,...]
    pallas_call x1, Pallas kernels: 18 us -> 19.5 us  [reduce_call(): pl.pallas_call(reduce_kernel, out_shape=jax.ShapeDtypeStruct((5, 2, 16),...]
where the time goes in v2:
time: 76.6 us; the launch traced here: 76.4 us
  Pallas kernels  71.3 us (93%)
  other arithmetic  3.13 us (4%)
  local copies, waits for them, and re-layouts  1.29 us (2%)
    pallas_call x1, Pallas kernels, exchange_call(): pl.pallas_call(exchange_kernel, out_shape=(jax.ShapeDtypeStruct((2, 2, 8,...  32.7 us
    pallas_call x1, Pallas kernels, reduce_call(): pl.pallas_call(reduce_kernel, out_shape=jax.ShapeDtypeStruct((5, 2, 16),...  19.5 us
    pallas_call x1, Pallas kernels, dft_call(): pl.pallas_call(dft_kernel, out_shape=jax.ShapeDtypeStruct((2560, LANES),...  11.7 us
    pallas_call x1, Pallas kernels, project_call(): pl.pallas_call(project_kernel, grid=(4,), out_shape=(jax.ShapeDtypeStruct...  7.39 us

profile of v2, /device:TPU:1, one launch (start us, length us, event | category | flops | bytes accessed | tf_op | source)
XLA Modules:
  0.0 76.4 jit_solution(14108427534859479522)
XLA Ops:
  0.6 0.9 %convert_reduce_fusion = s32[256]{0:T(256)S(1)} fusion(s32[256]{0:T(256)} %param.10), kind=kLoop, calls=%fused_computation | loop fusion | flops 327424 | bytes 2048 | tf_op jit(solution)/shard_map/reduce_sum | solution.py:494
  1.5 0.7 multiply_add_fusion
  2.2 0.0 copy-start
  2.2 0.9 %fusion.2 = (s32[4]{0:T(128)S(1)}, s32[4]{0:T(128)S(1)}) fusion(s32[256]{0:T(256)} %param.9, s32[256]{0:T(256)S(1)} %multiply_add_fusion, s32[4]{0:T(128)S(1)} %iota_add_fusion), kind=kLoop, calls=%fused_computation.6 | loop fusion | flops 5112 | bytes 2096 | tf_op jit(solution)/shard_map/reduce_sum | solution.py:502
  3.1 0.7 pad_add_fusion.meta
  3.8 0.0 copy-done
  3.8 11.7 %shard_map.86 = bf16[2560,128]{1,0:T(8,128)(2,1)} custom-call(bf16[80,40,2,128]{3,2,1,0:T(2,128)(2,1)} %bitcast.21, bf16[80,40,2,128]{3,2,1,0:T(2,128)(2,1)} %bitcast.22, s32[1,256]{1,0:T(1,128)} %bitcast.26, s32[1,256]{1,0:T(1,128)} %bitcast.25, bf16[640,640]{1,0:T(8,128)(2,1)} %constant.21.clone.order_ref, bf16[160,160]{1,0:T(8,128)(2,1)} %constant.22.clone.group_ref), custom_call_target="tpu_custom_call" | custom-call | tf_op jit(solution)/shard_map/pallas_call | solution.py:146
  15.5 32.7 %shard_map.87 = (bf16[2,2,8,16,5,2,128]{6,5,4,3,2,1,0:T(2,128)(2,1)}, bf16[4,1280,128]{2,1,0:T(8,128)(2,1)}) custom-call(bf16[128,2,5,2,128]{4,3,2,1,0:T(2,128)(2,1)} %bitcast.20, bf16[4,1280,640]{2,1,0:T(8,128)(2,1)} %table_ref.3), custom_call_target="tpu_custom_call" | custom-call | tf_op jit(solution)/shard_map/pallas_call | solution.py:256
  48.2 7.4 %shard_map.88 = (f32[4,2,16,2,640]{4,3,2,1,0:T(2,128)}, f32[32,1280]{1,0:T(8,128)}) custom-call(s32[9]{0:T(128)} %pad_add_fusion.meta, bf16[2,2,1280,128]{3,2,1,0:T(8,128)(2,1)} %bitcast.23, bf16[4,1280,640]{2,1,0:T(8,128)(2,1)} %table_ref.3, bf16[4,1280,128]{2,1,0:T(8,128)(2,1)} %get-tuple-element.7.edge_ref), custom_call_target="tpu_custom_call" | custom-call | tf_op jit(solution)/shard_map/pallas_call | solution.py:364
  55.6 19.5 %shard_map.89 = f32[5,2,16]{2,1,0:T(2,128)} custom-call(f32[32,1280]{1,0:T(8,128)} %get-tuple-element.9.energy_ref), custom_call_target="tpu_custom_call" | custom-call | tf_op jit(solution)/shard_map/pallas_call | solution.py:474
  75.1 1.3 %copy.14 = f32[2,16,5]{1,0,2:T(2,128)} copy(f32[2,16,5]{1,0,2:T(2,128)} %bitcast.24) | data formatting | bytes 1280
  (2 shorter events, 0.0 us)
Async XLA Ops:
  2.2 1.6 %copy-start = (s32[256]{0:T(256)}, s32[256]{0:T(256)S(1)}, u32[]{:S(2)}) copy-start(s32[256]{0:T(256)S(1)} %multiply_add_fusion) | copy-start | bytes 3076

commit v3 on v0

v3 whole, which is shorter than its diff:
```python
import math

import jax
import jax.numpy as jnp
from jax import lax
from jax.experimental import pallas as pl
from jax.experimental.pallas import tpu as pltpu
from jax.sharding import PartitionSpec as P

MESH = pl.DeviceIdType.MESH
BF16 = jnp.bfloat16
F32 = jnp.float32
I32 = jnp.int32
VMEM_BYTES = 56 * 1024 * 1024

NLON = 5120
LANES = 128
COARSE = NLON // LANES
ENTRIES = 256
ROWS = 10
HALF = 1280
COLS = 640
WIDE = COLS + LANES
CHUNK = 4
STEPS = COARSE // CHUNK

NT = (((1,), (1,)), ((), ()))


def iota(shape, axis):
    return lax.broadcasted_iota(I32, shape, axis)


def one_hot(hits):
    return hits.astype(F32).astype(BF16)


def row_order():
    wanted = iota((320, 320), 0)
    source = wanted % 2 * 160 + wanted // 16 % 2 * 80 + wanted // 2 % 8 * 10 + wanted // 32
    return one_hot(source == iota((320, 320), 1))


def group_order():
    source = iota((160, 160), 1)
    return one_hot(source % 16 * ROWS + source // 16 == iota((160, 160), 0))


def unit_waves(count, window, period):
    phase = iota((count, ENTRIES), 0).astype(F32) * window
    phase = phase - period * jnp.round(phase * (1.0 / period))
    angle = phase * (2.0 * math.pi / period)
    return jnp.cos(angle), jnp.sin(angle)


def stack(pieces, axis):
    return jnp.concatenate(pieces, axis=axis)


def kernel(
    wind_u, wind_v, window_ref, owner_ref, table_hbm, coeffs_hbm, spectra_ref,
    winds, coarse_cos, coarse_sin, fine_cos, fine_sin, highs, lows, total, split,
    outgoing, data, table, projected, coeffs, summed, send_a, recv_a, send_b, recv_b,
    wind_sems, table_sems, edge_sems, meet_core, meet_x, meet_y,
    out_sems, in_sems, core_send, core_recv, coeffs_sems, fold_send, fold_recv,
):
    me = lax.axis_index("wave")
    core = lax.axis_index("deg")
    other = 1 - core
    plane = me // 16
    inside = me % 16
    row = inside // 4
    column = inside % 4

    def along_z(step):
        return (plane + step) % 8 * 16 + inside

    def along_x(step):
        return plane * 16 + (row + step) % 4 * 4 + column

    def along_y(step):
        return plane * 16 + row * 4 + (column + step) % 4

    def signal(sem, where, side):
        pl.semaphore_signal(sem, inc=1, device_id=(where, side), device_id_type=MESH)

    def greet(sem, where, count):
        for step in range(1, count):
            signal(sem, where(step), core)

    barrier = pltpu.get_barrier_semaphore()
    greet(barrier, along_z, 8)
    greet(barrier, along_x, 4)
    greet(barrier, along_y, 4)
    signal(barrier, me, other)

    for f, ref in enumerate((wind_u, wind_v)):
        for tile in range(COARSE):
            pltpu.make_async_copy(ref.at[:, tile], winds.at[f, tile], wind_sems.at[f, tile // CHUNK]).start()

    def table_copy(slot):
        return pltpu.make_async_copy(
            table_hbm.at[slot], table.at[slot, :, pl.ds(0, COLS)], table_sems.at[slot]
        )

    for slot in range(4):
        table_copy(slot).start()

    window = window_ref[...].astype(F32)
    owner = owner_ref[...].astype(F32)
    owner_rows = jnp.broadcast_to(owner, (ENTRIES, ENTRIES))
    same = (jnp.transpose(owner_rows, (1, 0)) == owner_rows) & (
        iota((ENTRIES, ENTRIES), 0) < iota((ENTRIES, ENTRIES), 1)
    )
    rank = jnp.sum(same.astype(F32), axis=0, keepdims=True)
    placing = one_hot(owner_ref[...] == iota((128, ENTRIES), 0))
    rank_masks = [one_hot(rank == float(slot)) for slot in range(4)]

    cos_part, sin_part = unit_waves(COARSE, window, float(COARSE))
    coarse_cos[...] = cos_part
    coarse_sin[...] = sin_part
    cos_part, sin_part = unit_waves(LANES, window, float(NLON))
    fine_cos[...] = cos_part * (1.0 / NLON)
    fine_sin[...] = sin_part * (1.0 / NLON)

    def wind_chunk(f, chunk):
        part = winds.at[f, pl.ds(chunk * CHUNK, CHUNK)]
        pltpu.make_async_copy(part, part, wind_sems.at[f, chunk]).wait()
        return stack(
            [winds.at[f, chunk * CHUNK + inner].reshape(160, LANES)[...] for inner in range(CHUNK)], 1
        )

    def first_step(chunk, carry):
        cos_b = fine_cos[...]
        sin_b = fine_sin[...]
        for inner in range(CHUNK):
            tile = chunk * CHUNK + inner
            cos_a = coarse_cos[pl.ds(tile, 1), :]
            sin_a = coarse_sin[pl.ds(tile, 1), :]
            values = stack([cos_a * cos_b - sin_a * sin_b, -(sin_a * cos_b + cos_a * sin_b)], 1)
            high = values.astype(BF16)
            highs[chunk, LANES * inner : LANES * inner + LANES, :] = high
            lows[chunk, LANES * inner : LANES * inner + LANES, :] = (values - high.astype(F32)).astype(BF16)
        return second_step(0, chunk, carry)

    def second_step(f, chunk, carry):
        part = wind_chunk(f, chunk)
        total[...] += jnp.dot(part, highs[chunk], preferred_element_type=F32) + jnp.dot(
            part, lows[chunk], preferred_element_type=F32
        )
        return carry

    def publish(f):
        for tile in range(4):
            split[tile, :160] = total[:, LANES * tile : LANES * tile + LANES]
        north = stack([split[tile, pl.ds(0, 80, stride=2), :] for tile in range(4)], 1)
        south = stack([split[tile, pl.ds(1, 80, stride=2), :] for tile in range(4)], 1)
        even = (north + south).astype(BF16)
        odd = (north - south).astype(BF16)
        paired = stack([even[:, :ENTRIES], odd[:, :ENTRIES], even[:, ENTRIES:], odd[:, ENTRIES:]], 0)
        ordered = jnp.dot(row_order(), paired, preferred_element_type=F32).astype(BF16)
        blocks = stack(
            [
                ordered[32 * line : 32 * line + 32] * rank_masks[slot]
                for line in range(ROWS)
                for slot in range(4)
            ],
            0,
        )
        placed = lax.dot_general(placing, blocks, NT, preferred_element_type=F32).astype(BF16)
        stacked = stack(
            [
                stack(
                    [placed[16 * g : 16 * g + 16, LANES * line : LANES * line + LANES] for g in range(8)], 1
                )
                for line in range(ROWS)
            ],
            0,
        )
        result = jnp.dot(group_order(), stacked, preferred_element_type=F32).astype(BF16)
        flat = outgoing.at[f].reshape(HALF, LANES)
        for g in range(8):
            flat[160 * g : 160 * g + 160, :] = result[:, LANES * g : LANES * g + LANES]

    def partner(step):
        turn = step % 8
        away = (4 + (turn + 1) // 2 * (1 - 2 * (turn % 2)) + 8) % 8
        return (plane + away) % 8 * 16 + (row + step // 32) % 4 * 4 + (column + step // 8) % 4

    def own_copy(f):
        return pltpu.make_async_copy(
            outgoing.at[f, me], data.at[f, core, plane, inside], in_sems.at[f, 0]
        )

    def send_all(f):
        own_copy(f).start()

        def send(step, carry):
            target = partner(step)
            pltpu.make_async_remote_copy(
                src_ref=outgoing.at[f, target], dst_ref=data.at[f, core, plane, inside],
                send_sem=out_sems.at[f], recv_sem=in_sems.at[f, step // 8],
                device_id=(target, core), device_id_type=MESH,
            ).start()
            return carry

        lax.fori_loop(0, 7, send, 0)
        lax.fori_loop(8, 128, send, 0)

    def source_of(step):
        return (row + 4 - step // 4) % 4 * 4 + (column + 16 - step) % 4

    def forward(f, step):
        part = data.at[f, core, :, source_of(step)]
        return pltpu.make_async_remote_copy(
            src_ref=part, dst_ref=part, send_sem=core_send.at[f, step], recv_sem=core_recv.at[f, step],
            device_id=(me, other), device_id_type=MESH,
        )

    def forward_all(f):
        for step in range(16):
            part = data.at[f, core, :, source_of(step)]
            pltpu.make_async_copy(part, part, in_sems.at[f, step]).wait()
            forward(f, step).start()
        for step in range(16):
            arrived = data.at[f, other, :, source_of(step)]
            pltpu.make_async_copy(arrived, arrived, core_recv.at[f, step]).wait()

    unit = one_hot(iota((LANES, LANES), 0) == iota((LANES, LANES), 1))

    def project(f):
        turned = [
            lax.dot_general(
                unit, data.at[f, h].reshape(HALF, LANES)[...], NT, preferred_element_type=F32
            ).astype(BF16)
            for h in range(2)
        ]
        results = []
        for slot in range(4):
            if f == 0:
                table_copy(slot).wait()
            rows = stack([turned[h][32 * slot : 32 * slot + 32] for h in range(2)], 0)
            results.append(jnp.dot(rows, table[slot], preferred_element_type=F32))
        return results

    total[...] = jnp.zeros_like(total)
    lax.fori_loop(0, 4, first_step, 0)
    pl.semaphore_wait(barrier, 14)
    signal(meet_core, me, other)
    edge = pltpu.make_async_remote_copy(
        src_ref=table_hbm.at[:, :, pl.ds(pl.multiple_of(other * 512, LANES), LANES)],
        dst_ref=table.at[:, :, pl.ds(COLS, LANES)],
        send_sem=edge_sems.at[0], recv_sem=edge_sems.at[1],
        device_id=(me, other), device_id_type=MESH,
    )
    lax.fori_loop(4, 7, first_step, 0)
    pl.semaphore_wait(meet_core, 1)
    greet(meet_x, along_x, 4)
    lax.fori_loop(7, STEPS, first_step, 0)
    pl.semaphore_wait(meet_x, 3)
    greet(meet_y, along_y, 4)
    publish(0)
    pl.semaphore_wait(meet_y, 3)
    send_all(0)
    edge.start()

    total[...] = jnp.zeros_like(total)
    lax.fori_loop(0, STEPS, lambda chunk, carry: second_step(1, chunk, carry), 0)
    publish(1)
    send_all(1)

    forward_all(0)
    edge.wait()
    for slot, values in enumerate(project(0)):
        projected[slot] = values
    forward_all(1)
    second = project(1)

    shape = (32, COLS)
    col = iota(shape, 1)
    even_col = col % 2 == 0
    is_real = iota(shape, 0) % 2 == 0

    def times_unit(values):
        return jnp.where(is_real, -pltpu.roll(values, 31, 0), pltpu.roll(values, 1, 0))

    summed[...] = jnp.zeros_like(summed)
    for slot in range(4):
        hits = ((owner_ref[...] == me) & (rank == float(slot))).astype(F32)
        used = jnp.sum(hits)
        wave = jnp.where(used > 0, jnp.sum(hits * window), float(HALF)).astype(I32)
        last = jnp.where(used > 0, 2 * HALF - 1, -1)
        first_degree = wave + core * COLS
        live = first_degree + col <= last
        edge_live = wave + COLS - core <= last
        flows, before, after = [], [], []
        for values in (projected[slot], second[slot]):
            even = stack([values[0:16], values[32:48]], 0)
            odd = stack([values[16:32], values[48:64]], 0)
            flow = jnp.where(even_col, even[:, :COLS], odd[:, :COLS])
            flow = jnp.where(live, flow, 0.0)
            border = jnp.where(core == 0, even[:, COLS : COLS + 1], odd[:, WIDE - 1 :])
            border = jnp.where(edge_live, border, 0.0)
            flows.append(flow)
            before.append(
                jnp.where(col == 0, jnp.where(core == 1, border, 0.0), pltpu.roll(flow, 1, 1))
            )
            after.append(
                jnp.where(col == COLS - 1, jnp.where(core == 0, border, 0.0), pltpu.roll(flow, COLS - 1, 1))
            )
        degree_row = first_degree + iota((8, COLS), 1)
        degree = degree_row.astype(F32)
        next_row = degree_row + 1
        squared = wave * wave
        eps_here = jnp.sqrt((degree_row * degree_row - squared).astype(F32) / (4.0 * degree * degree - 1.0))
        eps_next = jnp.sqrt(
            (next_row * next_row - squared).astype(F32) / (4.0 * (degree + 1.0) * (degree + 1.0) - 1.0)
        )
        factor = lax.rsqrt(degree * (degree + 1.0))
        low_term = ((degree + 1.0) * eps_here * factor)[:1]
        high_term = (degree * eps_next * factor)[:1]
        wave_term = (wave.astype(F32) * factor)[:1]
        vorticity = wave_term * times_unit(flows[1]) + low_term * before[0] - high_term * after[0]
        divergence = wave_term * times_unit(flows[0]) - low_term * before[1] + high_term * after[1]
        for q, values in enumerate((vorticity, divergence)):
            values = jnp.where(live, values, 0.0)
            coeffs[slot, q] = values.reshape(16, 2, COLS)
            wide = stack([values * values, jnp.zeros(shape, F32)], 1)
            summed[32 * q : 32 * q + 32, :] += pltpu.roll(wide, first_degree - HALF, 1)
        pltpu.make_async_copy(coeffs.at[slot], coeffs_hbm.at[slot], coeffs_sems.at[slot]).start()

    for tile in range(HALF // LANES):
        base = 64 * (tile // 4)
        split[tile % 4, base : base + 64] = summed[:, LANES * tile : LANES * tile + LANES]
    pieces = []
    for tile in range(HALF // LANES):
        base = 64 * (tile // 4)
        pieces.append(
            split[tile % 4, pl.ds(base, 32, stride=2), :] + split[tile % 4, pl.ds(base + 1, 32, stride=2), :]
        )
    energy = stack(pieces, 1)

    def plane_partner(step):
        return (plane + step // 2) % 8, (core + step) % 2

    def inside_partner(step):
        return (inside + step // 2) % 16, (core + step) % 2

    lane = iota((8, 3 * LANES), 1)
    for there in range(8):
        for q in range(2):
            upper = energy[16 * q : 16 * q + 8, :]
            lower = energy[16 * q + 8 : 16 * q + 16, :]
            upper = pltpu.roll(upper, (HALF - 160 * there) % HALF, 1)[:, : 3 * LANES]
            lower = pltpu.roll(lower, (HALF + 160 - 160 * there) % HALF, 1)[:, : 3 * LANES]
            send_a[2 * there + q] = jnp.where(lane < 160, upper, lower)
    recv_a[2 * plane + core] = send_a[2 * plane + core]

    def send_planes(step, carry):
        there, side = plane_partner(step)
        pltpu.make_async_remote_copy(
            src_ref=send_a.at[2 * there + side], dst_ref=recv_a.at[2 * plane + core],
            send_sem=fold_send.at[0], recv_sem=fold_recv.at[0],
            device_id=(there * 16 + inside, side), device_id_type=MESH,
        ).start()
        return carry

    lax.fori_loop(1, 16, send_planes, 0)
    arrived = recv_a.at[pl.ds(0, 15)]
    pltpu.make_async_copy(arrived, arrived, fold_recv.at[0]).wait()
    chunk = recv_a[0]
    for index in range(1, 16):
        chunk = chunk + recv_a[index]
    narrow = lane[:, :LANES]
    for there in range(32):
        upper = pltpu.roll(chunk, (384 - 5 * there) % 384, 1)[:, :LANES]
        lower = pltpu.roll(chunk, 384 - 96 - 5 * there, 1)[:, :LANES]
        send_b[there] = jnp.where(narrow < 64, upper, lower)
    recv_b[2 * inside + core] = send_b[2 * inside + core]

    def send_inside(step, carry):
        there, side = inside_partner(step)
        pltpu.make_async_remote_copy(
            src_ref=send_b.at[2 * there + side], dst_ref=recv_b.at[2 * inside + core],
            send_sem=fold_send.at[1], recv_sem=fold_recv.at[1],
            device_id=(plane * 16 + there, side), device_id_type=MESH,
        ).start()
        return carry

    lax.fori_loop(1, 32, send_inside, 0)
    arrived = recv_b.at[pl.ds(0, 31)]
    pltpu.make_async_copy(arrived, arrived, fold_recv.at[1]).wait()
    for q in range(2):
        chunk = recv_b[q]
        for index in range(1, 16):
            chunk = chunk + recv_b[2 * index + q]
        turned = jnp.transpose(chunk * (1.0 / ENTRIES), (1, 0))
        spectra_ref[:, q, :] = stack([turned[:5], turned[64:69]], 1)

    for f in range(2):
        sent = outgoing.at[f, pl.ds(0, 127)]
        pltpu.make_async_copy(sent, sent, out_sems.at[f]).wait()
        for step in range(16):
            forward(f, step).wait_send()
    for slot in range(4):
        pltpu.make_async_copy(coeffs.at[slot], coeffs_hbm.at[slot], coeffs_sems.at[slot]).wait()
    sent = send_a.at[pl.ds(0, 15)]
    pltpu.make_async_copy(sent, sent, fold_send.at[0]).wait()
    sent = send_b.at[pl.ds(0, 31)]
    pltpu.make_async_copy(sent, sent, fold_send.at[1]).wait()


def tiles(wind):
    split = wind.transpose(0, 2, 1, 3).reshape(8, ROWS, 2, COARSE, LANES)
    return split.transpose(0, 1, 3, 2, 4).reshape(80, COARSE, 2, LANES)


def local(wind_u, wind_v, window_m, owner, legendre):
    vmem = pl.BlockSpec(memory_space=pltpu.VMEM)
    hbm = pl.BlockSpec(memory_space=pl.ANY)
    dma = pltpu.SemaphoreType.DMA
    regular = pltpu.SemaphoreType.REGULAR
    coeffs, spectra = pl.pallas_call(
        kernel,
        out_shape=(
            jax.ShapeDtypeStruct((4, 2, 16, 2, COLS), F32),
            jax.ShapeDtypeStruct((5, 2, 16), F32),
        ),
        in_specs=[hbm, hbm, vmem, vmem, hbm],
        out_specs=(hbm, vmem),
        scratch_shapes=[
            pltpu.VMEM((2, COARSE, 80, 2, LANES), BF16),
            pltpu.VMEM((COARSE, ENTRIES), F32),
            pltpu.VMEM((COARSE, ENTRIES), F32),
            pltpu.VMEM((LANES, ENTRIES), F32),
            pltpu.VMEM((LANES, ENTRIES), F32),
            pltpu.VMEM((STEPS, CHUNK * LANES, 2 * ENTRIES), BF16),
            pltpu.VMEM((STEPS, CHUNK * LANES, 2 * ENTRIES), BF16),
            pltpu.VMEM((160, 2 * ENTRIES), F32),
            pltpu.VMEM((4, 192, LANES), F32),
            pltpu.VMEM((2, 128, 5, 2, LANES), BF16),
            pltpu.VMEM((2, 2, 8, 16, 5, 2, LANES), BF16),
            pltpu.VMEM((4, HALF, WIDE), BF16),
            pltpu.VMEM((4, 64, WIDE), F32),
            pltpu.VMEM((4, 2, 16, 2, COLS), F32),
            pltpu.VMEM((64, HALF), F32),
            pltpu.VMEM((16, 8, 3 * LANES), F32),
            pltpu.VMEM((16, 8, 3 * LANES), F32),
            pltpu.VMEM((32, 8, LANES), F32),
            pltpu.VMEM((32, 8, LANES), F32),
            dma((2, STEPS)), dma((4,)), dma((2,)), regular, regular, regular,
            dma((2,)), dma((2, 16)), dma((2, 16)), dma((2, 16)), dma((4,)), dma((2,)), dma((2,)),
        ],
        compiler_params=pltpu.CompilerParams(
            collective_id=0, has_side_effects=True, vmem_limit_bytes=VMEM_BYTES
        ),
    )(tiles(wind_u), tiles(wind_v), window_m[None, :], owner[None, :], legendre)
    return (coeffs, spectra.transpose(1, 2, 0))


def solution(mesh):
    placed = (
        P("deg", None, "wave", None),
        P("deg", None, "wave", None),
        P(),
        P(),
        P("wave", None, "deg"),
    )
    return jax.shard_map(
        local,
        mesh=mesh,
        in_specs=placed,
        out_specs=(P("wave", None, None, None, "deg"), P(None, None, ("wave", "deg"))),
        check_vma=False,
    )
```

time: 471 us -> 59.8 us (0.13)
  waiting for transfers between devices: 288 us -> 0 us
  local copies, waits for them, and re-layouts: 90.6 us -> 3.29 us
  Pallas kernels: 0 us -> 55.7 us
  other arithmetic: 36.5 us -> 0 us
  starting transfers between devices: 21 us -> 0 us
  matrix products: 16.9 us -> 0 us
  between operations: 17 us -> 0.64 us
    unnamed x3 -> x0, waiting for transfers between devices: 258 us -> none
    all_to_all x2 -> x0, local copies, waits for them, and re-layouts: 66.3 us -> none  [local(): lax.all_to_all(outgoing, 'wave', split_axis=0, concat_axis=1, tiled=True)]
    pallas_call x0 -> x1, Pallas kernels: none -> 55.7 us  [local(): pl.pallas_call(kernel, out_shape=(jax.ShapeDtypeStruct((4, 2, 16, 2, COLS...]
    cos x1 -> x0, other arithmetic: 23.9 us -> none  [local(): jnp.cos(angles)]
    all_to_all x1 -> x0, waiting for transfers between devices: 20.8 us -> none  [local(): lax.all_to_all(outgoing, 'wave', split_axis=0, concat_axis=1, tiled=True)]
    dot_general x4 -> x0, matrix products: 16.9 us -> none  [the longest x1 6.97 us: local(): jnp.dot(wind_rows, table_high, preferred_element_type=jnp.float32)]
    all_to_all x1 -> x0, starting transfers between devices: 16.3 us -> none  [local(): lax.all_to_all(outgoing, 'wave', split_axis=0, concat_axis=1, tiled=True)]
    reshape x4 -> x0, local copies, waits for them, and re-layouts: 12.9 us -> none  [the longest x1 7.14 us: local(): wind_rows = jnp.stack([wind_u, wind_v], axis=1).reshape(-1, lon_count)]
  transfers between devices with their start and end apart: 5 -> 0, of which waited for: 3 -> 0; matrix products, arithmetic and copies ran while one was open for 0% -> 0% of each run, Pallas kernels for 0% -> 0%
where the time goes in v3:
time: 59.8 us; the launch traced here: 59.6 us
  Pallas kernels  55.7 us (93%)
  local copies, waits for them, and re-layouts  3.29 us (6%)
  between operations  0.64 us (1%)
    pallas_call x1, Pallas kernels, local(): pl.pallas_call(kernel, out_shape=(jax.ShapeDtypeStruct((4, 2, 16, 2, COLS...  55.7 us
    unnamed x2, local copies, waits for them, and re-layouts  3.29 us

profile of v3, /device:TPU:1, one launch (start us, length us, event | category | flops | bytes accessed | tf_op | source)
XLA Modules:
  0.0 59.6 jit_solution(9140924820007263906)
XLA Ops:
  0.6 55.7 %shard_map.68 = (f32[4,2,16,2,640]{4,3,2,1,0:T(2,128)}, f32[5,2,16]{2,1,0:T(2,128)}) custom-call(bf16[80,40,2,128]{3,2,1,0:T(2,128)(2,1)} %bitcast.17, bf16[80,40,2,128]{3,2,1,0:T(2,128)(2,1)} %bitcast.18, s32[1,256]{1,0:T(1,128)} %bitcast.20, s32[1,256]{1,0:T(1,128)} %bitcast.21, bf16[4,1280,640]{2,1,0:T(8,128)(2,1)} %table_hbm.1), custom_call_target="tpu_custom_call" | custom-call | tf_op jit(solution)/shard_map/pallas_call | solution.py:423
  56.3 2.0 %copy.11 = f32[4,2,16,2,640]{4,3,2,1,0:T(2,128)} copy(f32[4,2,16,2,640]{4,3,2,1,0:T(2,128)} %get-tuple-element.8) | data formatting | bytes 1310720
  58.3 1.3 %copy.12 = f32[2,16,5]{1,0,2:T(2,128)} copy(f32[2,16,5]{1,0,2:T(2,128)} %bitcast.19) | data formatting | bytes 1280

commit v4 on v3

v4 whole, which is shorter than its diff:
```python
import math

import jax
import jax.numpy as jnp
from jax import lax
from jax.experimental import pallas as pl
from jax.experimental.pallas import tpu as pltpu
from jax.sharding import PartitionSpec as P

MESH = pl.DeviceIdType.MESH
BF16 = jnp.bfloat16
F32 = jnp.float32
I32 = jnp.int32
VMEM_BYTES = 56 * 1024 * 1024

NLON = 5120
LANES = 128
COARSE = NLON // LANES
ENTRIES = 256
ROWS = 10
HALF = 1280
COLS = 640
WIDE = COLS + LANES
CHUNK = 4
STEPS = COARSE // CHUNK

NT = (((1,), (1,)), ((), ()))
FAR_PLANES = (4, 3, 5, 2, 6, 1, 7, 0)
FAR_LINES = (2, 1, 3, 0)


def iota(shape, axis):
    return lax.broadcasted_iota(I32, shape, axis)


def one_hot(hits):
    return hits.astype(F32).astype(BF16)


def row_order():
    wanted = iota((320, 320), 0)
    source = wanted % 2 * 160 + wanted // 16 % 2 * 80 + wanted // 2 % 8 * 10 + wanted // 32
    return one_hot(source == iota((320, 320), 1))


def group_order():
    source = iota((160, 160), 1)
    return one_hot(source % 16 * ROWS + source // 16 == iota((160, 160), 0))


def unit_waves(count, window, period):
    phase = iota((count, ENTRIES), 0).astype(F32) * window
    phase = phase - period * jnp.round(phase * (1.0 / period))
    angle = phase * (2.0 * math.pi / period)
    return jnp.cos(angle), jnp.sin(angle)


def stack(pieces, axis):
    return jnp.concatenate(pieces, axis=axis)


def kernel(
    wind_u, wind_v, window_ref, owner_ref, table_hbm, coeffs, spectra_ref,
    winds, coarse_cos, coarse_sin, fine_cos, fine_sin, highs, lows, total, split,
    outgoing, data, table, terms, partial, summed,
    fold_mask, fold_rows, paired_energy, other_energy, fold_out, fold_in, final,
    wind_sems, table_sems, edge_sems,
    out_sems, in_sems, core_send, core_recv, pair_sems, fold_sems, final_sems,
):
    me = lax.axis_index("wave")
    core = lax.axis_index("deg")
    other = 1 - core
    plane = me // 16
    inside = me % 16
    row = inside // 4
    column = inside % 4

    planes = [(plane + away) % 8 * 16 for away in FAR_PLANES]

    def everyone(action):
        def group(index, carry):
            turn_x = index // 4
            turn_y = index % 4
            away_x = 2 + (turn_x + 1) // 2 * (1 - 2 * (turn_x % 2))
            away_y = 2 + (turn_y + 1) // 2 * (1 - 2 * (turn_y % 2))
            base = (row + away_x) % 4 * 4 + (column + away_y) % 4
            for start in planes:
                action(start + base, index)
            return carry

        lax.fori_loop(0, 15, group, 0)
        for start in planes[:7]:
            action(start + inside, 15)

    def wind_copy(f, tile):
        ref = (wind_u, wind_v)[f]
        return pltpu.make_async_copy(ref.at[:, tile], winds.at[f, tile], wind_sems.at[f, tile // CHUNK])

    for tile in range(COARSE):
        wind_copy(0, tile).start()
    barrier = pltpu.get_barrier_semaphore()

    def greet(target, index):
        pl.semaphore_signal(barrier, inc=1, device_id=(target, core), device_id_type=MESH)

    everyone(greet)
    pl.semaphore_signal(barrier, inc=1, device_id=(me, other), device_id_type=MESH)

    def table_copy(slot):
        return pltpu.make_async_copy(
            table_hbm.at[slot], table.at[slot, :, pl.ds(0, COLS)], table_sems.at[slot]
        )

    window = window_ref[...].astype(F32)
    owner = owner_ref[...].astype(F32)
    owner_rows = jnp.broadcast_to(owner, (ENTRIES, ENTRIES))
    same = (jnp.transpose(owner_rows, (1, 0)) == owner_rows) & (
        iota((ENTRIES, ENTRIES), 0) < iota((ENTRIES, ENTRIES), 1)
    )
    rank = jnp.sum(same.astype(F32), axis=0, keepdims=True)
    placing = one_hot(owner_ref[...] == iota((128, ENTRIES), 0))
    rank_masks = [one_hot(rank == float(slot)) for slot in range(4)]

    cos_part, sin_part = unit_waves(COARSE, window, float(COARSE))
    coarse_cos[...] = cos_part
    coarse_sin[...] = sin_part
    cos_part, sin_part = unit_waves(LANES, window, float(NLON))
    fine_cos[...] = cos_part * (1.0 / NLON)
    fine_sin[...] = sin_part * (1.0 / NLON)

    def wind_chunk(f, chunk):
        part = winds.at[f, pl.ds(chunk * CHUNK, CHUNK)]
        pltpu.make_async_copy(part, part, wind_sems.at[f, chunk]).wait()
        return stack(
            [winds.at[f, chunk * CHUNK + inner].reshape(160, LANES)[...] for inner in range(CHUNK)], 1
        )

    def first_step(chunk, carry):
        for inner in range(CHUNK):
            wind_copy(1, chunk * CHUNK + inner).start()
        cos_b = fine_cos[...]
        sin_b = fine_sin[...]
        for inner in range(CHUNK):
            tile = chunk * CHUNK + inner
            cos_a = coarse_cos[pl.ds(tile, 1), :]
            sin_a = coarse_sin[pl.ds(tile, 1), :]
            values = stack([cos_a * cos_b - sin_a * sin_b, -(sin_a * cos_b + cos_a * sin_b)], 1)
            high = values.astype(BF16)
            highs[chunk, LANES * inner : LANES * inner + LANES, :] = high
            lows[chunk, LANES * inner : LANES * inner + LANES, :] = (values - high.astype(F32)).astype(BF16)
        return second_step(0, chunk, carry)

    def second_step(f, chunk, carry):
        part = wind_chunk(f, chunk)
        total[...] += jnp.dot(part, highs[chunk], preferred_element_type=F32) + jnp.dot(
            part, lows[chunk], preferred_element_type=F32
        )
        return carry

    def publish(f):
        for tile in range(4):
            split[tile, :160] = total[:, LANES * tile : LANES * tile + LANES]
        north = stack([split[tile, pl.ds(0, 80, stride=2), :] for tile in range(4)], 1)
        south = stack([split[tile, pl.ds(1, 80, stride=2), :] for tile in range(4)], 1)
        even = (north + south).astype(BF16)
        odd = (north - south).astype(BF16)
        paired = stack([even[:, :ENTRIES], odd[:, :ENTRIES], even[:, ENTRIES:], odd[:, ENTRIES:]], 0)
        ordered = jnp.dot(row_order(), paired, preferred_element_type=F32).astype(BF16)
        blocks = stack(
            [
                ordered[32 * line : 32 * line + 32] * rank_masks[slot]
                for line in range(ROWS)
                for slot in range(4)
            ],
            0,
        )
        placed = lax.dot_general(placing, blocks, NT, preferred_element_type=F32).astype(BF16)
        stacked = stack(
            [
                stack(
                    [placed[16 * g : 16 * g + 16, LANES * line : LANES * line + LANES] for g in range(8)], 1
                )
                for line in range(ROWS)
            ],
            0,
        )
        result = jnp.dot(group_order(), stacked, preferred_element_type=F32).astype(BF16)
        flat = outgoing.at[f].reshape(HALF, LANES)
        for g in range(8):
            flat[160 * g : 160 * g + 160, :] = result[:, LANES * g : LANES * g + LANES]

    def own_copy(f):
        return pltpu.make_async_copy(
            outgoing.at[f, me], data.at[f, core, plane, inside], in_sems.at[f, 15]
        )

    def send_all(f):
        own_copy(f).start()

        def send(target, index):
            pltpu.make_async_remote_copy(
                src_ref=outgoing.at[f, target], dst_ref=data.at[f, core, plane, inside],
                send_sem=out_sems.at[f], recv_sem=in_sems.at[f, index],
                device_id=(target, core), device_id_type=MESH,
            ).start()

        everyone(send)

    def source_of(step):
        return (row + 4 - FAR_LINES[step // 4]) % 4 * 4 + (column + 4 - FAR_LINES[step % 4]) % 4

    def forward(f, step):
        part = data.at[f, core, :, source_of(step)]
        return pltpu.make_async_remote_copy(
            src_ref=part, dst_ref=part, send_sem=core_send.at[f, step], recv_sem=core_recv.at[f, step],
            device_id=(me, other), device_id_type=MESH,
        )

    def forward_all(f):
        for step in range(16):
            part = data.at[f, core, :, source_of(step)]
            pltpu.make_async_copy(part, part, in_sems.at[f, step]).wait()
            forward(f, step).start()
        for step in range(16):
            arrived = data.at[f, other, :, source_of(step)]
            pltpu.make_async_copy(arrived, arrived, core_recv.at[f, step]).wait()

    unit = one_hot(iota((LANES, LANES), 0) == iota((LANES, LANES), 1))

    def project(f):
        turned = [
            lax.dot_general(
                unit, data.at[f, h].reshape(HALF, LANES)[...], NT, preferred_element_type=F32
            ).astype(BF16)
            for h in range(2)
        ]
        results = []
        for slot in range(4):
            if f == 0:
                table_copy(slot).wait()
            rows = stack([turned[h][32 * slot : 32 * slot + 32] for h in range(2)], 0)
            results.append(jnp.dot(rows, table[slot], preferred_element_type=F32))
        return results

    total[...] = jnp.zeros_like(total)
    lax.fori_loop(0, STEPS, first_step, 0)
    publish(0)
    pl.semaphore_wait(barrier, 128)
    send_all(0)
    edge = pltpu.make_async_remote_copy(
        src_ref=table_hbm.at[:, :, pl.ds(pl.multiple_of(other * 512, LANES), LANES)],
        dst_ref=table.at[:, :, pl.ds(COLS, LANES)],
        send_sem=edge_sems.at[0], recv_sem=edge_sems.at[1],
        device_id=(me, other), device_id_type=MESH,
    )
    for slot in range(4):
        table_copy(slot).start()
    edge.start()

    total[...] = jnp.zeros_like(total)
    lax.fori_loop(0, STEPS, lambda chunk, carry: second_step(1, chunk, carry), 0)
    publish(1)
    send_all(1)

    fold_lane = iota((HALF, 2 * LANES), 1)
    fold_turn = fold_lane % 64 // 8
    fold_mask[...] = one_hot(
        (iota((HALF, 2 * LANES), 0) % 10 == fold_lane % LANES // 64 * 5 + fold_turn) & (fold_turn < 5)
    )
    fold_rows[...] = one_hot(iota((LANES, HALF), 1) // 10 == iota((LANES, HALF), 0))
    spread_lane = iota((16, 2 * LANES), 1)
    spread = one_hot(spread_lane // LANES * 8 + spread_lane % 8 == iota((16, 2 * LANES), 0))

    forward_all(0)
    edge.wait()
    first = project(0)

    shape = (32, COLS)
    col = iota(shape, 1)
    even_col = col % 2 == 0
    is_real = iota(shape, 0) % 2 == 0

    def times_unit(values):
        return jnp.where(is_real, -pltpu.roll(values, 31, 0), pltpu.roll(values, 1, 0))

    def neighbours(slot, values):
        wave, last = waves[slot]
        even = stack([values[0:16], values[32:48]], 0)
        odd = stack([values[16:32], values[48:64]], 0)
        flow = jnp.where(even_col, even[:, :COLS], odd[:, :COLS])
        flow = jnp.where(wave + core * COLS + col <= last, flow, 0.0)
        border = jnp.where(core == 0, even[:, COLS : COLS + 1], odd[:, WIDE - 1 :])
        border = jnp.where(wave + COLS - core <= last, border, 0.0)
        before = jnp.where(col == 0, jnp.where(core == 1, border, 0.0), pltpu.roll(flow, 1, 1))
        after = jnp.where(
            col == COLS - 1, jnp.where(core == 0, border, 0.0), pltpu.roll(flow, COLS - 1, 1)
        )
        return before, flow, after

    waves = []
    for slot in range(4):
        hits = ((owner_ref[...] == me) & (rank == float(slot))).astype(F32)
        used = jnp.sum(hits)
        wave = jnp.where(used > 0, jnp.sum(hits * window), float(HALF)).astype(I32)
        waves.append((wave, jnp.where(used > 0, 2 * HALF - 1, -1)))
        degree_row = wave + core * COLS + iota((8, COLS), 1)
        degree = degree_row.astype(F32)
        next_row = degree_row + 1
        squared = wave * wave
        eps_here = jnp.sqrt((degree_row * degree_row - squared).astype(F32) / (4.0 * degree * degree - 1.0))
        eps_next = jnp.sqrt(
            (next_row * next_row - squared).astype(F32) / (4.0 * (degree + 1.0) * (degree + 1.0) - 1.0)
        )
        factor = lax.rsqrt(degree * (degree + 1.0))
        terms[slot, 0] = (degree + 1.0) * eps_here * factor
        terms[slot, 1] = degree * eps_next * factor
        terms[slot, 2] = wave.astype(F32) * factor
        before, flow, after = neighbours(slot, first[slot])
        partial[slot, 0] = terms[slot, 0, :1] * before - terms[slot, 1, :1] * after
        partial[slot, 1] = terms[slot, 2, :1] * times_unit(flow)
    summed[...] = jnp.zeros_like(summed)

    forward_all(1)
    second = project(1)
    for slot in range(4):
        wave, last = waves[slot]
        first_degree = wave + core * COLS
        live = first_degree + col <= last
        before, flow, after = neighbours(slot, second[slot])
        vorticity = partial[slot, 0] + terms[slot, 2, :1] * times_unit(flow)
        divergence = partial[slot, 1] - terms[slot, 0, :1] * before + terms[slot, 1, :1] * after
        vorticity = jnp.where(live, vorticity, 0.0)
        divergence = jnp.where(live, divergence, 0.0)
        coeffs[slot, 0] = vorticity.reshape(16, 2, COLS)
        coeffs[slot, 1] = divergence.reshape(16, 2, COLS)
        vorticity = vorticity * vorticity
        divergence = divergence * divergence
        energy = jnp.where(
            is_real,
            vorticity + pltpu.roll(vorticity, 31, 0),
            divergence + pltpu.roll(divergence, 1, 0),
        )
        wide = stack([energy, jnp.zeros(shape, F32)], 1)
        summed[...] += pltpu.roll(wide, first_degree - HALF, 1)

    for tile in range(HALF // LANES):
        split[tile % 4, 0:32] = summed[:, LANES * tile : LANES * tile + LANES]
        for q in range(2):
            paired_energy[q, :, LANES * tile : LANES * tile + LANES] = split[tile % 4, pl.ds(q, 16, stride=2), :]

    def to_other(src, dst, sems):
        copy = pltpu.make_async_remote_copy(
            src_ref=src, dst_ref=dst, send_sem=sems.at[0], recv_sem=sems.at[1],
            device_id=(me, other), device_id_type=MESH,
        )
        copy.start()
        copy.wait()

    to_other(paired_energy.at[other], other_energy, pair_sems)
    chip_energy = paired_energy[core] + other_energy[...]
    turned = jnp.transpose(chip_energy, (1, 0)).astype(BF16)
    placed = jnp.dot(turned, spread, preferred_element_type=F32).astype(BF16) * fold_mask[...]
    messages = jnp.dot(fold_rows[...], placed, preferred_element_type=F32)
    for half in range(2):
        fold_out[:, half, :] = messages[:, LANES * half : LANES * half + LANES]
    fold_in[me] = fold_out[me]

    def send_fold(target, index):
        pltpu.make_async_remote_copy(
            src_ref=fold_out.at[target], dst_ref=fold_in.at[me],
            send_sem=fold_sems.at[0], recv_sem=fold_sems.at[1],
            device_id=(target, core), device_id_type=MESH,
        ).start()

    everyone(send_fold)
    arrived = fold_in.at[pl.ds(0, 127)]
    pltpu.make_async_copy(arrived, arrived, fold_sems.at[1]).wait()
    lines = fold_in.reshape(2 * LANES, LANES)
    folded = lines[0:8, :]
    for index in range(1, 32):
        folded = folded + lines[8 * index : 8 * index + 8, :]
    final[core] = folded[0:2] + folded[2:4] + folded[4:6] + folded[6:8]
    to_other(final.at[core], final.at[core], final_sems)
    halves = []
    for half in range(2):
        values = final[:, half, :] * (1.0 / ENTRIES)
        halves.append(jnp.where(core == 1, pltpu.roll(values, 64, 1), values))
    for index in range(5):
        spectra_ref[index] = stack([values[:, 8 * index : 8 * index + 8] for values in halves], 1)

    for f in range(2):
        sent = outgoing.at[f, pl.ds(0, 127)]
        pltpu.make_async_copy(sent, sent, out_sems.at[f]).wait()
        for step in range(16):
            forward(f, step).wait_send()
    sent = fold_out.at[pl.ds(0, 127)]
    pltpu.make_async_copy(sent, sent, fold_sems.at[0]).wait()


def tiles(wind):
    split = wind.transpose(0, 2, 1, 3).reshape(8, ROWS, 2, COARSE, LANES)
    return split.transpose(0, 1, 3, 2, 4).reshape(80, COARSE, 2, LANES)


def local(wind_u, wind_v, window_m, owner, legendre):
    vmem = pl.BlockSpec(memory_space=pltpu.VMEM)
    hbm = pl.BlockSpec(memory_space=pl.ANY)
    dma = pltpu.SemaphoreType.DMA
    coeffs, spectra = pl.pallas_call(
        kernel,
        out_shape=(pltpu.VMEM((4, 2, 16, 2, COLS), F32), pltpu.VMEM((5, 2, 16), F32)),
        in_specs=[hbm, hbm, vmem, vmem, hbm],
        out_specs=(vmem, vmem),
        scratch_shapes=[
            pltpu.VMEM((2, COARSE, 80, 2, LANES), BF16),
            pltpu.VMEM((COARSE, ENTRIES), F32),
            pltpu.VMEM((COARSE, ENTRIES), F32),
            pltpu.VMEM((LANES, ENTRIES), F32),
            pltpu.VMEM((LANES, ENTRIES), F32),
            pltpu.VMEM((STEPS, CHUNK * LANES, 2 * ENTRIES), BF16),
            pltpu.VMEM((STEPS, CHUNK * LANES, 2 * ENTRIES), BF16),
            pltpu.VMEM((160, 2 * ENTRIES), F32),
            pltpu.VMEM((4, 192, LANES), F32),
            pltpu.VMEM((2, 128, 5, 2, LANES), BF16),
            pltpu.VMEM((2, 2, 8, 16, 5, 2, LANES), BF16),
            pltpu.VMEM((4, HALF, WIDE), BF16),
            pltpu.VMEM((4, 3, 8, COLS), F32),
            pltpu.VMEM((4, 2, 32, COLS), F32),
            pltpu.VMEM((32, HALF), F32),
            pltpu.VMEM((HALF, 2 * LANES), BF16),
            pltpu.VMEM((LANES, HALF), BF16),
            pltpu.VMEM((2, 16, HALF), F32),
            pltpu.VMEM((16, HALF), F32),
            pltpu.VMEM((LANES, 2, LANES), F32),
            pltpu.VMEM((LANES, 2, LANES), F32),
            pltpu.VMEM((2, 2, LANES), F32),
            dma((2, STEPS)), dma((4,)), dma((2,)),
            dma((2,)), dma((2, 16)), dma((2, 16)), dma((2, 16)),
            dma((2,)), dma((2,)), dma((2,)),
        ],
        compiler_params=pltpu.CompilerParams(
            collective_id=0, has_side_effects=True, vmem_limit_bytes=VMEM_BYTES
        ),
    )(tiles(wind_u), tiles(wind_v), window_m[None, :], owner[None, :], legendre)
    return (coeffs, spectra.transpose(1, 2, 0))


def solution(mesh):
    placed = (
        P("deg", None, "wave", None),
        P("deg", None, "wave", None),
        P(),
        P(),
        P("wave", None, "deg"),
    )
    return jax.shard_map(
        local,
        mesh=mesh,
        in_specs=placed,
        out_specs=(P("wave", None, None, None, "deg"), P(None, None, ("wave", "deg"))),
        check_vma=False,
    )
```

time: 59.8 us -> 51.7 us (0.86)
  Pallas kernels: 55.7 us -> 49.5 us
  local copies, waits for them, and re-layouts: 3.29 us -> 1.43 us
    pallas_call x1, Pallas kernels: 55.7 us -> 49.5 us  [local(): pl.pallas_call(kernel, out_shape=(pltpu.VMEM((4, 2, 16, 2, COLS), F32), p...]
    unnamed x2, local copies, waits for them, and re-layouts: 3.29 us -> 1.43 us
where the time goes in v4:
time: 51.7 us; the launch traced here: 51.6 us
  Pallas kernels  49.5 us (96%)
  local copies, waits for them, and re-layouts  1.43 us (3%)
  between operations  0.64 us (1%)
    pallas_call x1, Pallas kernels, local(): pl.pallas_call(kernel, out_shape=(pltpu.VMEM((4, 2, 16, 2, COLS), F32), p...  49.5 us
    unnamed x2, local copies, waits for them, and re-layouts  1.43 us

profile of v4, /device:TPU:1, one launch (start us, length us, event | category | flops | bytes accessed | tf_op | source)
XLA Modules:
  0.0 51.6 jit_solution(12992541944817647950)
XLA Ops:
  0.6 49.5 %shard_map.68 = (f32[4,2,16,2,640]{4,3,2,1,0:T(2,128)S(1)}, f32[5,2,16]{2,1,0:T(2,128)S(1)}) custom-call(bf16[80,40,2,128]{3,2,1,0:T(2,128)(2,1)} %bitcast.18, bf16[80,40,2,128]{3,2,1,0:T(2,128)(2,1)} %bitcast.19, s32[1,256]{1,0:T(1,128)} %bitcast.20, s32[1,256]{1,0:T(1,128)} %bitcast.21, bf16[4,1280,640]{2,1,0:T(8,128)(2,1)} %table_hbm.1), custom_call_target="tpu_custom_call" | custom-call | tf_op jit(solution)/shard_map/pallas_call | solution.py:409
  50.1 0.8 %copy.11 = f32[4,2,16,2,640]{4,3,2,1,0:T(2,128)} copy(f32[4,2,16,2,640]{4,3,2,1,0:T(2,128)S(1)} %get-tuple-element.6) | data formatting | bytes 1310720
  51.0 0.6 %copy.12 = f32[2,16,5]{1,0,2:T(2,128)} copy(f32[2,16,5]{1,0,2:T(2,128)S(1)} %bitcast.17) | data formatting | bytes 1280

commit v5 on v4

--- a/solution.py
+++ b/solution.py
@@ -21,7 +21,7 @@
 HALF = 1280
 COLS = 640
 WIDE = COLS + LANES
-CHUNK = 4
+CHUNK = 20
 STEPS = COARSE // CHUNK
 
 NT = (((1,), (1,)), ((), ()))
@@ -61,7 +61,7 @@
 
 def kernel(
     wind_u, wind_v, window_ref, owner_ref, table_hbm, coeffs, spectra_ref,
-    winds, coarse_cos, coarse_sin, fine_cos, fine_sin, highs, lows, total, split,
+    winds, coarse_cos, coarse_sin, fine_cos, fine_sin, waves_table, total, split,
     outgoing, data, table, terms, partial, summed,
     fold_mask, fold_rows, paired_energy, other_energy, fold_out, fold_in, final,
     wind_sems, table_sems, edge_sems,
@@ -77,13 +77,16 @@
 
     planes = [(plane + away) % 8 * 16 for away in FAR_PLANES]
 
+    def group_base(index):
+        turn_x = index // 4
+        turn_y = index % 4
+        away_x = 2 + (turn_x + 1) // 2 * (1 - 2 * (turn_x % 2))
+        away_y = 2 + (turn_y + 1) // 2 * (1 - 2 * (turn_y % 2))
+        return (row + away_x) % 4 * 4 + (column + away_y) % 4
+
     def everyone(action):
         def group(index, carry):
-            turn_x = index // 4
-            turn_y = index % 4
-            away_x = 2 + (turn_x + 1) // 2 * (1 - 2 * (turn_x % 2))
-            away_y = 2 + (turn_y + 1) // 2 * (1 - 2 * (turn_y % 2))
-            base = (row + away_x) % 4 * 4 + (column + away_y) % 4
+            base = group_base(index)
             for start in planes:
                 action(start + base, index)
             return carry
@@ -100,11 +103,15 @@
         wind_copy(0, tile).start()
     barrier = pltpu.get_barrier_semaphore()
 
-    def greet(target, index):
-        pl.semaphore_signal(barrier, inc=1, device_id=(target, core), device_id_type=MESH)
-
-    everyone(greet)
-    pl.semaphore_signal(barrier, inc=1, device_id=(me, other), device_id_type=MESH)
+    def greet_group(index, carry):
+        base = group_base(index)
+        for start in planes[:7]:
+            pl.semaphore_signal(barrier, inc=1, device_id=(start + base, core), device_id_type=MESH)
+        side = jnp.where(base == inside, other, core)
+        pl.semaphore_signal(barrier, inc=1, device_id=(planes[7] + base, side), device_id_type=MESH)
+        return carry
+
+    lax.fori_loop(0, 16, greet_group, 0)
 
     def table_copy(slot):
         return pltpu.make_async_copy(
@@ -135,27 +142,35 @@
             [winds.at[f, chunk * CHUNK + inner].reshape(160, LANES)[...] for inner in range(CHUNK)], 1
         )
 
-    def first_step(chunk, carry):
-        for inner in range(CHUNK):
-            wind_copy(1, chunk * CHUNK + inner).start()
+    def prepare(step, carry):
         cos_b = fine_cos[...]
         sin_b = fine_sin[...]
-        for inner in range(CHUNK):
-            tile = chunk * CHUNK + inner
+        for inner in range(5):
+            tile = step * 5 + inner
+            wind_copy(1, tile).start()
             cos_a = coarse_cos[pl.ds(tile, 1), :]
             sin_a = coarse_sin[pl.ds(tile, 1), :]
             values = stack([cos_a * cos_b - sin_a * sin_b, -(sin_a * cos_b + cos_a * sin_b)], 1)
             high = values.astype(BF16)
-            highs[chunk, LANES * inner : LANES * inner + LANES, :] = high
-            lows[chunk, LANES * inner : LANES * inner + LANES, :] = (values - high.astype(F32)).astype(BF16)
-        return second_step(0, chunk, carry)
-
-    def second_step(f, chunk, carry):
-        part = wind_chunk(f, chunk)
-        total[...] += jnp.dot(part, highs[chunk], preferred_element_type=F32) + jnp.dot(
-            part, lows[chunk], preferred_element_type=F32
-        )
+            first = (tile // CHUNK * CHUNK + tile) * LANES
+            waves_table[pl.ds(pl.multiple_of(first, LANES), LANES), :] = high
+            second = first + CHUNK * LANES
+            low = (values - high.astype(F32)).astype(BF16)
+            waves_table[pl.ds(pl.multiple_of(second, LANES), LANES), :] = low
         return carry
+
+    def transform(f):
+        def step(chunk, carry):
+            part = wind_chunk(f, chunk)
+            depth = 2 * CHUNK * LANES
+            here = pl.ds(pl.multiple_of(chunk * depth, depth), depth)
+            total[...] += jnp.dot(
+                stack([part, part], 1), waves_table[here, :], preferred_element_type=F32
+            )
+            return carry
+
+        total[...] = jnp.zeros_like(total)
+        lax.fori_loop(0, STEPS, step, 0)
 
     def publish(f):
         for tile in range(4):
@@ -216,34 +231,33 @@
             device_id=(me, other), device_id_type=MESH,
         )
 
-    def forward_all(f):
-        for step in range(16):
+    def forward_start(f, steps):
+        for step in steps:
             part = data.at[f, core, :, source_of(step)]
             pltpu.make_async_copy(part, part, in_sems.at[f, step]).wait()
             forward(f, step).start()
+
+    def forward_wait(f):
         for step in range(16):
             arrived = data.at[f, other, :, source_of(step)]
             pltpu.make_async_copy(arrived, arrived, core_recv.at[f, step]).wait()
 
     unit = one_hot(iota((LANES, LANES), 0) == iota((LANES, LANES), 1))
 
-    def project(f):
-        turned = [
+    def turn(f):
+        return [
             lax.dot_general(
                 unit, data.at[f, h].reshape(HALF, LANES)[...], NT, preferred_element_type=F32
             ).astype(BF16)
             for h in range(2)
         ]
-        results = []
-        for slot in range(4):
-            if f == 0:
-                table_copy(slot).wait()
-            rows = stack([turned[h][32 * slot : 32 * slot + 32] for h in range(2)], 0)
-            results.append(jnp.dot(rows, table[slot], preferred_element_type=F32))
-        return results
-
-    total[...] = jnp.zeros_like(total)
-    lax.fori_loop(0, STEPS, first_step, 0)
+
+    def project(turned, slot):
+        rows = stack([turned[h][32 * slot : 32 * slot + 32] for h in range(2)], 0)
+        return jnp.dot(rows, table[slot], preferred_element_type=F32)
+
+    lax.fori_loop(0, 8, prepare, 0)
+    transform(0)
     publish(0)
     pl.semaphore_wait(barrier, 128)
     send_all(0)
@@ -257,8 +271,7 @@
         table_copy(slot).start()
     edge.start()
 
-    total[...] = jnp.zeros_like(total)
-    lax.fori_loop(0, STEPS, lambda chunk, carry: second_step(1, chunk, carry), 0)
+    transform(1)
     publish(1)
     send_all(1)
 
@@ -271,9 +284,12 @@
     spread_lane = iota((16, 2 * LANES), 1)
     spread = one_hot(spread_lane // LANES * 8 + spread_lane % 8 == iota((16, 2 * LANES), 0))
 
-    forward_all(0)
+    forward_start(0, range(16))
+    forward_wait(0)
     edge.wait()
-    first = project(0)
+    for slot in range(4):
+        table_copy(slot).wait()
+    turned = turn(0)
 
     shape = (32, COLS)
     col = iota(shape, 1)
@@ -298,7 +314,9 @@
         return before, flow, after
 
     waves = []
+    ready = (range(0, 5), range(5, 9), range(9, 12), range(12, 13))
     for slot in range(4):
+        forward_start(1, ready[slot])
         hits = ((owner_ref[...] == me) & (rank == float(slot))).astype(F32)
         used = jnp.sum(hits)
         wave = jnp.where(used > 0, jnp.sum(hits * window), float(HALF)).astype(I32)
@@ -315,18 +333,19 @@
         terms[slot, 0] = (degree + 1.0) * eps_here * factor
         terms[slot, 1] = degree * eps_next * factor
         terms[slot, 2] = wave.astype(F32) * factor
-        before, flow, after = neighbours(slot, first[slot])
+        before, flow, after = neighbours(slot, project(turned, slot))
         partial[slot, 0] = terms[slot, 0, :1] * before - terms[slot, 1, :1] * after
         partial[slot, 1] = terms[slot, 2, :1] * times_unit(flow)
     summed[...] = jnp.zeros_like(summed)
 
-    forward_all(1)
-    second = project(1)
+    forward_start(1, range(13, 16))
+    forward_wait(1)
+    turned = turn(1)
     for slot in range(4):
         wave, last = waves[slot]
         first_degree = wave + core * COLS
         live = first_degree + col <= last
-        before, flow, after = neighbours(slot, second[slot])
+        before, flow, after = neighbours(slot, project(turned, slot))
         vorticity = partial[slot, 0] + terms[slot, 2, :1] * times_unit(flow)
         divergence = partial[slot, 1] - terms[slot, 0, :1] * before + terms[slot, 1, :1] * after
         vorticity = jnp.where(live, vorticity, 0.0)
@@ -358,8 +377,8 @@
 
     to_other(paired_energy.at[other], other_energy, pair_sems)
     chip_energy = paired_energy[core] + other_energy[...]
-    turned = jnp.transpose(chip_energy, (1, 0)).astype(BF16)
-    placed = jnp.dot(turned, spread, preferred_element_type=F32).astype(BF16) * fold_mask[...]
+    upright = jnp.transpose(chip_energy, (1, 0)).astype(BF16)
+    placed = jnp.dot(upright, spread, preferred_element_type=F32).astype(BF16) * fold_mask[...]
     messages = jnp.dot(fold_rows[...], placed, preferred_element_type=F32)
     for half in range(2):
         fold_out[:, half, :] = messages[:, LANES * half : LANES * half + LANES]
@@ -417,8 +436,7 @@
             pltpu.VMEM((COARSE, ENTRIES), F32),
             pltpu.VMEM((LANES, ENTRIES), F32),
             pltpu.VMEM((LANES, ENTRIES), F32),
-            pltpu.VMEM((STEPS, CHUNK * LANES, 2 * ENTRIES), BF16),
-            pltpu.VMEM((STEPS, CHUNK * LANES, 2 * ENTRIES), BF16),
+            pltpu.VMEM((2 * NLON, 2 * ENTRIES), BF16),
             pltpu.VMEM((160, 2 * ENTRIES), F32),
             pltpu.VMEM((4, 192, LANES), F32),
             pltpu.VMEM((2, 128, 5, 2, LANES), BF16),

time: 51.7 us -> 52 us (level)
  no operation moved by 1% of the time
where the time goes in v5:
time: 52 us; the launch traced here: 51.9 us
  Pallas kernels  49.9 us (96%)
  local copies, waits for them, and re-layouts  1.43 us (3%)
  between operations  0.64 us (1%)
    pallas_call x1, Pallas kernels, local(): pl.pallas_call(kernel, out_shape=(pltpu.VMEM((4, 2, 16, 2, COLS), F32), p...  49.9 us
    unnamed x2, local copies, waits for them, and re-layouts  1.43 us

profile of v5, /device:TPU:1, one launch (start us, length us, event | category | flops | bytes accessed | tf_op | source)
XLA Modules:
  0.0 51.9 jit_solution(5196747173436169904)
XLA Ops:
  0.6 49.9 %shard_map.68 = (f32[4,2,16,2,640]{4,3,2,1,0:T(2,128)S(1)}, f32[5,2,16]{2,1,0:T(2,128)S(1)}) custom-call(bf16[80,40,2,128]{3,2,1,0:T(2,128)(2,1)} %bitcast.18, bf16[80,40,2,128]{3,2,1,0:T(2,128)(2,1)} %bitcast.19, s32[1,256]{1,0:T(1,128)} %bitcast.20, s32[1,256]{1,0:T(1,128)} %bitcast.21, bf16[4,1280,640]{2,1,0:T(8,128)(2,1)} %table_hbm.1), custom_call_target="tpu_custom_call" | custom-call | tf_op jit(solution)/shard_map/pallas_call | solution.py:428
  50.5 0.8 %copy.11 = f32[4,2,16,2,640]{4,3,2,1,0:T(2,128)} copy(f32[4,2,16,2,640]{4,3,2,1,0:T(2,128)S(1)} %get-tuple-element.6) | data formatting | bytes 1310720
  51.3 0.6 %copy.12 = f32[2,16,5]{1,0,2:T(2,128)} copy(f32[2,16,5]{1,0,2:T(2,128)S(1)} %bitcast.17) | data formatting | bytes 1280

commit v6 on v5

--- a/solution.py
+++ b/solution.py
@@ -20,7 +20,6 @@
 ROWS = 10
 HALF = 1280
 COLS = 640
-WIDE = COLS + LANES
 CHUNK = 20
 STEPS = COARSE // CHUNK
 
@@ -62,10 +61,10 @@
 def kernel(
     wind_u, wind_v, window_ref, owner_ref, table_hbm, coeffs, spectra_ref,
     winds, coarse_cos, coarse_sin, fine_cos, fine_sin, waves_table, total, split,
-    outgoing, data, table, terms, partial, summed,
-    fold_mask, fold_rows, paired_energy, other_energy, fold_out, fold_in, final,
-    wind_sems, table_sems, edge_sems,
-    out_sems, in_sems, core_send, core_recv, pair_sems, fold_sems, final_sems,
+    outgoing, data, table, terms, partial, summed, coeffs_out,
+    fold_mask, fold_rows, fold_out, fold_in, final,
+    wind_sems, table_sems, share_send, share_recv, meet,
+    out_sems, in_sems, coeffs_send, coeffs_recv, fold_sems, final_sems,
 ):
     me = lax.axis_index("wave")
     core = lax.axis_index("deg")
@@ -101,22 +100,40 @@
 
     for tile in range(COARSE):
         wind_copy(0, tile).start()
+    def greet_plane(sem):
+        def greet(step, carry):
+            there = plane * 16 + (inside + step) % 16
+            pl.semaphore_signal(sem, inc=1, device_id=(there, core), device_id_type=MESH)
+            return carry
+
+        lax.fori_loop(1, 16, greet, 0)
+
+    def greet_line(step, carry):
+        there = (plane + step) % 8 * 16 + inside
+        pl.semaphore_signal(barrier, inc=1, device_id=(there, core), device_id_type=MESH)
+        return carry
+
     barrier = pltpu.get_barrier_semaphore()
-
-    def greet_group(index, carry):
-        base = group_base(index)
-        for start in planes[:7]:
-            pl.semaphore_signal(barrier, inc=1, device_id=(start + base, core), device_id_type=MESH)
-        side = jnp.where(base == inside, other, core)
-        pl.semaphore_signal(barrier, inc=1, device_id=(planes[7] + base, side), device_id_type=MESH)
-        return carry
-
-    lax.fori_loop(0, 16, greet_group, 0)
+    pl.semaphore_signal(barrier, inc=1, device_id=(me, other), device_id_type=MESH)
+    lax.fori_loop(1, 8, greet_line, 0)
+    greet_plane(barrier)
+
+    own_half = pl.ds(pl.multiple_of(core * COLS, LANES), COLS)
 
     def table_copy(slot):
-        return pltpu.make_async_copy(
-            table_hbm.at[slot], table.at[slot, :, pl.ds(0, COLS)], table_sems.at[slot]
-        )
+        return pltpu.make_async_copy(table_hbm.at[slot], table.at[slot, :, own_half], table_sems.at[slot])
+
+    def table_share(slot):
+        return pltpu.make_async_remote_copy(
+            src_ref=table_hbm.at[slot], dst_ref=table.at[slot, :, own_half],
+            send_sem=share_send.at[slot], recv_sem=share_recv.at[slot],
+            device_id=(me, other), device_id_type=MESH,
+        )
+
+    def table_ready(slot):
+        table_copy(slot).wait()
+        half = table.at[slot, :, pl.ds(pl.multiple_of(other * COLS, LANES), COLS)]
+        pltpu.make_async_copy(half, half, share_recv.at[slot]).wait()
 
     window = window_ref[...].astype(F32)
     owner = owner_ref[...].astype(F32)
@@ -206,7 +223,7 @@
 
     def own_copy(f):
         return pltpu.make_async_copy(
-            outgoing.at[f, me], data.at[f, core, plane, inside], in_sems.at[f, 15]
+            outgoing.at[f, me], data.at[f, plane, inside], in_sems.at[f, 15]
         )
 
     def send_all(f):
@@ -214,66 +231,44 @@
 
         def send(target, index):
             pltpu.make_async_remote_copy(
-                src_ref=outgoing.at[f, target], dst_ref=data.at[f, core, plane, inside],
+                src_ref=outgoing.at[f, target], dst_ref=data.at[f, plane, inside],
                 send_sem=out_sems.at[f], recv_sem=in_sems.at[f, index],
                 device_id=(target, core), device_id_type=MESH,
             ).start()
 
         everyone(send)
 
-    def source_of(step):
-        return (row + 4 - FAR_LINES[step // 4]) % 4 * 4 + (column + 4 - FAR_LINES[step % 4]) % 4
-
-    def forward(f, step):
-        part = data.at[f, core, :, source_of(step)]
-        return pltpu.make_async_remote_copy(
-            src_ref=part, dst_ref=part, send_sem=core_send.at[f, step], recv_sem=core_recv.at[f, step],
-            device_id=(me, other), device_id_type=MESH,
-        )
-
-    def forward_start(f, steps):
-        for step in steps:
-            part = data.at[f, core, :, source_of(step)]
+    def arrive(f):
+        for step in range(16):
+            source = (row + 4 - FAR_LINES[step // 4]) % 4 * 4 + (column + 4 - FAR_LINES[step % 4]) % 4
+            part = data.at[f, :, source]
             pltpu.make_async_copy(part, part, in_sems.at[f, step]).wait()
-            forward(f, step).start()
-
-    def forward_wait(f):
-        for step in range(16):
-            arrived = data.at[f, other, :, source_of(step)]
-            pltpu.make_async_copy(arrived, arrived, core_recv.at[f, step]).wait()
 
     unit = one_hot(iota((LANES, LANES), 0) == iota((LANES, LANES), 1))
 
     def turn(f):
-        return [
-            lax.dot_general(
-                unit, data.at[f, h].reshape(HALF, LANES)[...], NT, preferred_element_type=F32
-            ).astype(BF16)
-            for h in range(2)
-        ]
+        return lax.dot_general(
+            unit, data.at[f].reshape(HALF, LANES)[...], NT, preferred_element_type=F32
+        ).astype(BF16)
 
     def project(turned, slot):
-        rows = stack([turned[h][32 * slot : 32 * slot + 32] for h in range(2)], 0)
-        return jnp.dot(rows, table[slot], preferred_element_type=F32)
+        return jnp.dot(turned[32 * slot : 32 * slot + 32], table[slot], preferred_element_type=F32)
 
     lax.fori_loop(0, 8, prepare, 0)
+    pl.semaphore_wait(barrier, 23)
+    greet_plane(meet)
     transform(0)
     publish(0)
-    pl.semaphore_wait(barrier, 128)
+    pl.semaphore_wait(meet, 15)
     send_all(0)
-    edge = pltpu.make_async_remote_copy(
-        src_ref=table_hbm.at[:, :, pl.ds(pl.multiple_of(other * 512, LANES), LANES)],
-        dst_ref=table.at[:, :, pl.ds(COLS, LANES)],
-        send_sem=edge_sems.at[0], recv_sem=edge_sems.at[1],
-        device_id=(me, other), device_id_type=MESH,
-    )
     for slot in range(4):
         table_copy(slot).start()
-    edge.start()
 
     transform(1)
     publish(1)
     send_all(1)
+    for slot in range(4):
+        table_share(slot).start()
 
     fold_lane = iota((HALF, 2 * LANES), 1)
     fold_turn = fold_lane % 64 // 8
@@ -281,47 +276,33 @@
         (iota((HALF, 2 * LANES), 0) % 10 == fold_lane % LANES // 64 * 5 + fold_turn) & (fold_turn < 5)
     )
     fold_rows[...] = one_hot(iota((LANES, HALF), 1) // 10 == iota((LANES, HALF), 0))
+    spread_row = iota((16, 2 * LANES), 0)
     spread_lane = iota((16, 2 * LANES), 1)
-    spread = one_hot(spread_lane // LANES * 8 + spread_lane % 8 == iota((16, 2 * LANES), 0))
-
-    forward_start(0, range(16))
-    forward_wait(0)
-    edge.wait()
-    for slot in range(4):
-        table_copy(slot).wait()
-    turned = turn(0)
-
-    shape = (32, COLS)
+    spread = one_hot((spread_row % 2 == spread_lane // LANES) & (spread_row // 2 == spread_lane % 8))
+
+    shape = (16, HALF)
     col = iota(shape, 1)
     even_col = col % 2 == 0
     is_real = iota(shape, 0) % 2 == 0
 
     def times_unit(values):
-        return jnp.where(is_real, -pltpu.roll(values, 31, 0), pltpu.roll(values, 1, 0))
+        return jnp.where(is_real, -pltpu.roll(values, 15, 0), pltpu.roll(values, 1, 0))
 
     def neighbours(slot, values):
         wave, last = waves[slot]
-        even = stack([values[0:16], values[32:48]], 0)
-        odd = stack([values[16:32], values[48:64]], 0)
-        flow = jnp.where(even_col, even[:, :COLS], odd[:, :COLS])
-        flow = jnp.where(wave + core * COLS + col <= last, flow, 0.0)
-        border = jnp.where(core == 0, even[:, COLS : COLS + 1], odd[:, WIDE - 1 :])
-        border = jnp.where(wave + COLS - core <= last, border, 0.0)
-        before = jnp.where(col == 0, jnp.where(core == 1, border, 0.0), pltpu.roll(flow, 1, 1))
-        after = jnp.where(
-            col == COLS - 1, jnp.where(core == 0, border, 0.0), pltpu.roll(flow, COLS - 1, 1)
-        )
+        flow = jnp.where(even_col, values[:16], values[16:])
+        flow = jnp.where(wave + col <= last, flow, 0.0)
+        before = jnp.where(col == 0, 0.0, pltpu.roll(flow, 1, 1))
+        after = jnp.where(col == HALF - 1, 0.0, pltpu.roll(flow, HALF - 1, 1))
         return before, flow, after
 
     waves = []
-    ready = (range(0, 5), range(5, 9), range(9, 12), range(12, 13))
-    for slot in range(4):
-        forward_start(1, ready[slot])
+    for slot in range(4):
         hits = ((owner_ref[...] == me) & (rank == float(slot))).astype(F32)
         used = jnp.sum(hits)
         wave = jnp.where(used > 0, jnp.sum(hits * window), float(HALF)).astype(I32)
         waves.append((wave, jnp.where(used > 0, 2 * HALF - 1, -1)))
-        degree_row = wave + core * COLS + iota((8, COLS), 1)
+        degree_row = wave + iota((8, HALF), 1)
         degree = degree_row.astype(F32)
         next_row = degree_row + 1
         squared = wave * wave
@@ -333,51 +314,50 @@
         terms[slot, 0] = (degree + 1.0) * eps_here * factor
         terms[slot, 1] = degree * eps_next * factor
         terms[slot, 2] = wave.astype(F32) * factor
+    summed[...] = jnp.zeros_like(summed)
+
+    arrive(0)
+    turned = turn(0)
+    for slot in range(4):
+        table_ready(slot)
         before, flow, after = neighbours(slot, project(turned, slot))
         partial[slot, 0] = terms[slot, 0, :1] * before - terms[slot, 1, :1] * after
         partial[slot, 1] = terms[slot, 2, :1] * times_unit(flow)
-    summed[...] = jnp.zeros_like(summed)
-
-    forward_start(1, range(13, 16))
-    forward_wait(1)
+
+    own_levels = pl.ds(core * 8, 8)
+
+    def hand_over(slot):
+        return pltpu.make_async_remote_copy(
+            src_ref=coeffs_out.at[slot], dst_ref=coeffs.at[slot, :, own_levels],
+            send_sem=coeffs_send.at[slot], recv_sem=coeffs_recv.at[slot],
+            device_id=(me, other), device_id_type=MESH,
+        )
+
+    arrive(1)
     turned = turn(1)
     for slot in range(4):
         wave, last = waves[slot]
-        first_degree = wave + core * COLS
-        live = first_degree + col <= last
+        live = wave + col <= last
         before, flow, after = neighbours(slot, project(turned, slot))
         vorticity = partial[slot, 0] + terms[slot, 2, :1] * times_unit(flow)
         divergence = partial[slot, 1] - terms[slot, 0, :1] * before + terms[slot, 1, :1] * after
         vorticity = jnp.where(live, vorticity, 0.0)
         divergence = jnp.where(live, divergence, 0.0)
-        coeffs[slot, 0] = vorticity.reshape(16, 2, COLS)
-        coeffs[slot, 1] = divergence.reshape(16, 2, COLS)
+        for q, values in enumerate((vorticity, divergence)):
+            lower, upper = values[:, :COLS], values[:, COLS:]
+            coeffs[slot, q, own_levels] = jnp.where(core == 0, lower, upper).reshape(8, 2, COLS)
+            coeffs_out[slot, q] = jnp.where(core == 0, upper, lower).reshape(8, 2, COLS)
+        hand_over(slot).start()
         vorticity = vorticity * vorticity
         divergence = divergence * divergence
         energy = jnp.where(
             is_real,
-            vorticity + pltpu.roll(vorticity, 31, 0),
+            vorticity + pltpu.roll(vorticity, 15, 0),
             divergence + pltpu.roll(divergence, 1, 0),
         )
-        wide = stack([energy, jnp.zeros(shape, F32)], 1)
-        summed[...] += pltpu.roll(wide, first_degree - HALF, 1)
-
-    for tile in range(HALF // LANES):
-        split[tile % 4, 0:32] = summed[:, LANES * tile : LANES * tile + LANES]
-        for q in range(2):
-            paired_energy[q, :, LANES * tile : LANES * tile + LANES] = split[tile % 4, pl.ds(q, 16, stride=2), :]
-
-    def to_other(src, dst, sems):
-        copy = pltpu.make_async_remote_copy(
-            src_ref=src, dst_ref=dst, send_sem=sems.at[0], recv_sem=sems.at[1],
-            device_id=(me, other), device_id_type=MESH,
-        )
-        copy.start()
-        copy.wait()
-
-    to_other(paired_energy.at[other], other_energy, pair_sems)
-    chip_energy = paired_energy[core] + other_energy[...]
-    upright = jnp.transpose(chip_energy, (1, 0)).astype(BF16)
+        summed[...] += pltpu.roll(energy, wave - HALF, 1)
+
+    upright = jnp.transpose(summed[...], (1, 0)).astype(BF16)
     placed = jnp.dot(upright, spread, preferred_element_type=F32).astype(BF16) * fold_mask[...]
     messages = jnp.dot(fold_rows[...], placed, preferred_element_type=F32)
     for half in range(2):
@@ -399,21 +379,29 @@
     for index in range(1, 32):
         folded = folded + lines[8 * index : 8 * index + 8, :]
     final[core] = folded[0:2] + folded[2:4] + folded[4:6] + folded[6:8]
-    to_other(final.at[core], final.at[core], final_sems)
+    swap = pltpu.make_async_remote_copy(
+        src_ref=final.at[core], dst_ref=final.at[core],
+        send_sem=final_sems.at[0], recv_sem=final_sems.at[1],
+        device_id=(me, other), device_id_type=MESH,
+    )
+    swap.start()
+    for f in range(2):
+        sent = outgoing.at[f, pl.ds(0, 127)]
+        pltpu.make_async_copy(sent, sent, out_sems.at[f]).wait()
+    for slot in range(4):
+        table_share(slot).wait_send()
+        hand_over(slot).wait_send()
+        half = coeffs.at[slot, :, pl.ds(other * 8, 8)]
+        pltpu.make_async_copy(half, half, coeffs_recv.at[slot]).wait()
+    sent = fold_out.at[pl.ds(0, 127)]
+    pltpu.make_async_copy(sent, sent, fold_sems.at[0]).wait()
+    swap.wait()
     halves = []
     for half in range(2):
-        values = final[:, half, :] * (1.0 / ENTRIES)
+        values = final[half] * (1.0 / ENTRIES)
         halves.append(jnp.where(core == 1, pltpu.roll(values, 64, 1), values))
     for index in range(5):
         spectra_ref[index] = stack([values[:, 8 * index : 8 * index + 8] for values in halves], 1)
-
-    for f in range(2):
-        sent = outgoing.at[f, pl.ds(0, 127)]
-        pltpu.make_async_copy(sent, sent, out_sems.at[f]).wait()
-        for step in range(16):
-            forward(f, step).wait_send()
-    sent = fold_out.at[pl.ds(0, 127)]
-    pltpu.make_async_copy(sent, sent, fold_sems.at[0]).wait()
 
 
 def tiles(wind):
@@ -440,21 +428,19 @@
             pltpu.VMEM((160, 2 * ENTRIES), F32),
             pltpu.VMEM((4, 192, LANES), F32),
             pltpu.VMEM((2, 128, 5, 2, LANES), BF16),
-            pltpu.VMEM((2, 2, 8, 16, 5, 2, LANES), BF16),
-            pltpu.VMEM((4, HALF, WIDE), BF16),
-            pltpu.VMEM((4, 3, 8, COLS), F32),
-            pltpu.VMEM((4, 2, 32, COLS), F32),
-            pltpu.VMEM((32, HALF), F32),
+            pltpu.VMEM((2, 8, 16, 5, 2, LANES), BF16),
+            pltpu.VMEM((4, HALF, HALF), BF16),
+            pltpu.VMEM((4, 3, 8, HALF), F32),
+            pltpu.VMEM((4, 2, 16, HALF), F32),
+            pltpu.VMEM((16, HALF), F32),
+            pltpu.VMEM((4, 2, 8, 2, COLS), F32),
             pltpu.VMEM((HALF, 2 * LANES), BF16),
             pltpu.VMEM((LANES, HALF), BF16),
-            pltpu.VMEM((2, 16, HALF), F32),
-            pltpu.VMEM((16, HALF), F32),
             pltpu.VMEM((LANES, 2, LANES), F32),
             pltpu.VMEM((LANES, 2, LANES), F32),
             pltpu.VMEM((2, 2, LANES), F32),
-            dma((2, STEPS)), dma((4,)), dma((2,)),
-            dma((2,)), dma((2, 16)), dma((2, 16)), dma((2, 16)),
-            dma((2,)), dma((2,)), dma((2,)),
+            dma((2, STEPS)), dma((4,)), dma((4,)), dma((4,)), pltpu.SemaphoreType.REGULAR,
+            dma((2,)), dma((2, 16)), dma((4,)), dma((4,)), dma((2,)), dma((2,)),
         ],
         compiler_params=pltpu.CompilerParams(
             collective_id=0, has_side_effects=True, vmem_limit_bytes=VMEM_BYTES

time: 52 us -> 49.1 us (0.944)
  Pallas kernels: 49.9 us -> 46.9 us
    pallas_call x1, Pallas kernels: 49.9 us -> 46.9 us  [local(): pl.pallas_call(kernel, out_shape=(pltpu.VMEM((4, 2, 16, 2, COLS), F32), p...]
where the time goes in v6:
time: 49.1 us; the launch traced here: 49 us
  Pallas kernels  46.9 us (96%)
  local copies, waits for them, and re-layouts  1.43 us (3%)
  between operations  0.64 us (1%)
    pallas_call x1, Pallas kernels, local(): pl.pallas_call(kernel, out_shape=(pltpu.VMEM((4, 2, 16, 2, COLS), F32), p...  46.9 us
    unnamed x2, local copies, waits for them, and re-layouts  1.43 us

profile of v6, /device:TPU:1, one launch (start us, length us, event | category | flops | bytes accessed | tf_op | source)
XLA Modules:
  0.0 49.0 jit_solution(245185663174708209)
XLA Ops:
  0.6 46.9 %shard_map.68 = (f32[4,2,16,2,640]{4,3,2,1,0:T(2,128)S(1)}, f32[5,2,16]{2,1,0:T(2,128)S(1)}) custom-call(bf16[80,40,2,128]{3,2,1,0:T(2,128)(2,1)} %bitcast.18, bf16[80,40,2,128]{3,2,1,0:T(2,128)(2,1)} %bitcast.19, s32[1,256]{1,0:T(1,128)} %bitcast.20, s32[1,256]{1,0:T(1,128)} %bitcast.21, bf16[4,1280,640]{2,1,0:T(8,128)(2,1)} %table_hbm.1), custom_call_target="tpu_custom_call" | custom-call | tf_op jit(solution)/shard_map/pallas_call | solution.py:416
  47.6 0.8 %copy.11 = f32[4,2,16,2,640]{4,3,2,1,0:T(2,128)} copy(f32[4,2,16,2,640]{4,3,2,1,0:T(2,128)S(1)} %get-tuple-element.6) | data formatting | bytes 1310720
  48.4 0.6 %copy.12 = f32[2,16,5]{1,0,2:T(2,128)} copy(f32[2,16,5]{1,0,2:T(2,128)S(1)} %bitcast.17) | data formatting | bytes 1280

commit v7 on v6

--- a/solution.py
+++ b/solution.py
@@ -136,15 +136,6 @@
         pltpu.make_async_copy(half, half, share_recv.at[slot]).wait()
 
     window = window_ref[...].astype(F32)
-    owner = owner_ref[...].astype(F32)
-    owner_rows = jnp.broadcast_to(owner, (ENTRIES, ENTRIES))
-    same = (jnp.transpose(owner_rows, (1, 0)) == owner_rows) & (
-        iota((ENTRIES, ENTRIES), 0) < iota((ENTRIES, ENTRIES), 1)
-    )
-    rank = jnp.sum(same.astype(F32), axis=0, keepdims=True)
-    placing = one_hot(owner_ref[...] == iota((128, ENTRIES), 0))
-    rank_masks = [one_hot(rank == float(slot)) for slot in range(4)]
-
     cos_part, sin_part = unit_waves(COARSE, window, float(COARSE))
     coarse_cos[...] = cos_part
     coarse_sin[...] = sin_part
@@ -177,17 +168,21 @@
         return carry
 
     def transform(f):
-        def step(chunk, carry):
+        def step(chunk):
             part = wind_chunk(f, chunk)
             depth = 2 * CHUNK * LANES
-            here = pl.ds(pl.multiple_of(chunk * depth, depth), depth)
-            total[...] += jnp.dot(
-                stack([part, part], 1), waves_table[here, :], preferred_element_type=F32
+            product = jnp.dot(
+                stack([part, part], 1),
+                waves_table[depth * chunk : depth * chunk + depth, :],
+                preferred_element_type=F32,
             )
-            return carry
-
-        total[...] = jnp.zeros_like(total)
-        lax.fori_loop(0, STEPS, step, 0)
+            if chunk == 0:
+                total[...] = product
+            else:
+                total[...] += product
+
+        for chunk in range(STEPS):
+            step(chunk)
 
     def publish(f):
         for tile in range(4):
@@ -254,9 +249,19 @@
     def project(turned, slot):
         return jnp.dot(turned[32 * slot : 32 * slot + 32], table[slot], preferred_element_type=F32)
 
-    lax.fori_loop(0, 8, prepare, 0)
+    lax.fori_loop(0, 4, prepare, 0)
     pl.semaphore_wait(barrier, 23)
     greet_plane(meet)
+    lax.fori_loop(4, 8, prepare, 0)
+    owner = owner_ref[...].astype(F32)
+    owner_rows = jnp.broadcast_to(owner, (ENTRIES, ENTRIES))
+    same = (jnp.transpose(owner_rows, (1, 0)) == owner_rows) & (
+        iota((ENTRIES, ENTRIES), 0) < iota((ENTRIES, ENTRIES), 1)
+    )
+    rank = jnp.sum(same.astype(F32), axis=0, keepdims=True)
+    placing = one_hot(owner_ref[...] == iota((128, ENTRIES), 0))
+    rank_masks = [one_hot(rank == float(slot)) for slot in range(4)]
+
     transform(0)
     publish(0)
     pl.semaphore_wait(meet, 15)
@@ -276,6 +281,8 @@
         (iota((HALF, 2 * LANES), 0) % 10 == fold_lane % LANES // 64 * 5 + fold_turn) & (fold_turn < 5)
     )
     fold_rows[...] = one_hot(iota((LANES, HALF), 1) // 10 == iota((LANES, HALF), 0))
+    pair_row = iota((2 * LANES, 2 * LANES), 0)
+    interleave = one_hot(pair_row % 2 * LANES + pair_row // 2 == iota((2 * LANES, 2 * LANES), 1))
     spread_row = iota((16, 2 * LANES), 0)
     spread_lane = iota((16, 2 * LANES), 1)
     spread = one_hot((spread_row % 2 == spread_lane // LANES) & (spread_row // 2 == spread_lane % 8))
@@ -360,8 +367,11 @@
     upright = jnp.transpose(summed[...], (1, 0)).astype(BF16)
     placed = jnp.dot(upright, spread, preferred_element_type=F32).astype(BF16) * fold_mask[...]
     messages = jnp.dot(fold_rows[...], placed, preferred_element_type=F32)
-    for half in range(2):
-        fold_out[:, half, :] = messages[:, LANES * half : LANES * half + LANES]
+    messages = messages.astype(BF16)
+    messages = stack([messages[:, :LANES], messages[:, LANES:]], 0)
+    fold_out.reshape(2 * LANES, LANES)[...] = jnp.dot(
+        interleave, messages, preferred_element_type=F32
+    ).astype(BF16)
     fold_in[me] = fold_out[me]
 
     def send_fold(target, index):
@@ -374,10 +384,10 @@
     everyone(send_fold)
     arrived = fold_in.at[pl.ds(0, 127)]
     pltpu.make_async_copy(arrived, arrived, fold_sems.at[1]).wait()
-    lines = fold_in.reshape(2 * LANES, LANES)
-    folded = lines[0:8, :]
+    lines = fold_in.reshape(2 * LANES, LANES)[...].astype(F32)
+    folded = lines[0:8]
     for index in range(1, 32):
-        folded = folded + lines[8 * index : 8 * index + 8, :]
+        folded = folded + lines[8 * index : 8 * index + 8]
     final[core] = folded[0:2] + folded[2:4] + folded[4:6] + folded[6:8]
     swap = pltpu.make_async_remote_copy(
         src_ref=final.at[core], dst_ref=final.at[core],
@@ -436,8 +446,8 @@
             pltpu.VMEM((4, 2, 8, 2, COLS), F32),
             pltpu.VMEM((HALF, 2 * LANES), BF16),
             pltpu.VMEM((LANES, HALF), BF16),
-            pltpu.VMEM((LANES, 2, LANES), F32),
-            pltpu.VMEM((LANES, 2, LANES), F32),
+            pltpu.VMEM((LANES, 2, LANES), BF16),
+            pltpu.VMEM((LANES, 2, LANES), BF16),
             pltpu.VMEM((2, 2, LANES), F32),
             dma((2, STEPS)), dma((4,)), dma((4,)), dma((4,)), pltpu.SemaphoreType.REGULAR,
             dma((2,)), dma((2, 16)), dma((4,)), dma((4,)), dma((2,)), dma((2,)),

time: 49.1 us -> 49.3 us (level)
  no operation moved by 1% of the time
where the time goes in v7:
time: 49.3 us; the launch traced here: 49.2 us
  Pallas kernels  47.2 us (96%)
  local copies, waits for them, and re-layouts  1.43 us (3%)
  between operations  0.64 us (1%)
    pallas_call x1, Pallas kernels, local(): pl.pallas_call(kernel, out_shape=(pltpu.VMEM((4, 2, 16, 2, COLS), F32), p...  47.2 us
    unnamed x2, local copies, waits for them, and re-layouts  1.43 us

profile of v7, /device:TPU:1, one launch (start us, length us, event | category | flops | bytes accessed | tf_op | source)
XLA Modules:
  0.0 49.2 jit_solution(16817188323255358860)
XLA Ops:
  0.6 47.2 %shard_map.68 = (f32[4,2,16,2,640]{4,3,2,1,0:T(2,128)S(1)}, f32[5,2,16]{2,1,0:T(2,128)S(1)}) custom-call(bf16[80,40,2,128]{3,2,1,0:T(2,128)(2,1)} %bitcast.18, bf16[80,40,2,128]{3,2,1,0:T(2,128)(2,1)} %bitcast.19, s32[1,256]{1,0:T(1,128)} %bitcast.20, s32[1,256]{1,0:T(1,128)} %bitcast.21, bf16[4,1280,640]{2,1,0:T(8,128)(2,1)} %table_hbm.1), custom_call_target="tpu_custom_call" | custom-call | tf_op jit(solution)/shard_map/pallas_call | solution.py:426
  47.8 0.8 %copy.11 = f32[4,2,16,2,640]{4,3,2,1,0:T(2,128)} copy(f32[4,2,16,2,640]{4,3,2,1,0:T(2,128)S(1)} %get-tuple-element.6) | data formatting | bytes 1310720
  48.6 0.6 %copy.12 = f32[2,16,5]{1,0,2:T(2,128)} copy(f32[2,16,5]{1,0,2:T(2,128)S(1)} %bitcast.17) | data formatting | bytes 1280

commit v8 on v6

--- a/solution.py
+++ b/solution.py
@@ -24,6 +24,7 @@
 STEPS = COARSE // CHUNK
 
 NT = (((1,), (1,)), ((), ()))
+BATCHES = ((0, 0, 4), (0, 4, 6), (1, 0, 10))
 FAR_PLANES = (4, 3, 5, 2, 6, 1, 7, 0)
 FAR_LINES = (2, 1, 3, 0)
 
@@ -36,15 +37,17 @@
     return hits.astype(F32).astype(BF16)
 
 
-def row_order():
-    wanted = iota((320, 320), 0)
-    source = wanted % 2 * 160 + wanted // 16 % 2 * 80 + wanted // 2 % 8 * 10 + wanted // 32
-    return one_hot(source == iota((320, 320), 1))
-
-
-def group_order():
-    source = iota((160, 160), 1)
-    return one_hot(source % 16 * ROWS + source // 16 == iota((160, 160), 0))
+def row_order(rows):
+    wanted = iota((32 * rows, 32 * rows), 0)
+    source = (
+        wanted % 2 * (16 * rows) + wanted // 16 % 2 * (8 * rows) + wanted // 2 % 8 * rows + wanted // 32
+    )
+    return one_hot(source == iota((32 * rows, 32 * rows), 1))
+
+
+def group_order(rows):
+    source = iota((16 * rows, 16 * rows), 1)
+    return one_hot(source % 16 * rows + source // 16 == iota((16 * rows, 16 * rows), 0))
 
 
 def unit_waves(count, window, period):
@@ -60,12 +63,14 @@
 
 def kernel(
     wind_u, wind_v, window_ref, owner_ref, table_hbm, coeffs, spectra_ref,
-    winds, coarse_cos, coarse_sin, fine_cos, fine_sin, waves_table, total, split,
-    outgoing, data, table, terms, partial, summed, coeffs_out,
+    winds_a, winds_b, winds_c, coarse_cos, coarse_sin, fine_cos, fine_sin, waves_table, total, split,
+    outgoing_a, outgoing_b, outgoing_c, data, table, terms, partial, summed, coeffs_out,
     fold_mask, fold_rows, fold_out, fold_in, final,
     wind_sems, table_sems, share_send, share_recv, meet,
     out_sems, in_sems, coeffs_send, coeffs_recv, fold_sems, final_sems,
 ):
+    winds = (winds_a, winds_b, winds_c)
+    outgoing = (outgoing_a, outgoing_b, outgoing_c)
     me = lax.axis_index("wave")
     core = lax.axis_index("deg")
     other = 1 - core
@@ -94,9 +99,12 @@
         for start in planes[:7]:
             action(start + inside, 15)
 
-    def wind_copy(f, tile):
+    def wind_copy(batch, tile):
+        f, first, rows = BATCHES[batch]
         ref = (wind_u, wind_v)[f]
-        return pltpu.make_async_copy(ref.at[:, tile], winds.at[f, tile], wind_sems.at[f, tile // CHUNK])
+        return pltpu.make_async_copy(
+            ref.at[:, pl.ds(first, rows), tile], winds[batch].at[tile], wind_sems.at[batch, tile // CHUNK]
+        )
 
     for tile in range(COARSE):
         wind_copy(0, tile).start()
@@ -152,11 +160,12 @@
     fine_cos[...] = cos_part * (1.0 / NLON)
     fine_sin[...] = sin_part * (1.0 / NLON)
 
-    def wind_chunk(f, chunk):
-        part = winds.at[f, pl.ds(chunk * CHUNK, CHUNK)]
-        pltpu.make_async_copy(part, part, wind_sems.at[f, chunk]).wait()
+    def wind_chunk(batch, chunk):
+        lines = 16 * BATCHES[batch][2]
+        part = winds[batch].at[pl.ds(chunk * CHUNK, CHUNK)]
+        pltpu.make_async_copy(part, part, wind_sems.at[batch, chunk]).wait()
         return stack(
-            [winds.at[f, chunk * CHUNK + inner].reshape(160, LANES)[...] for inner in range(CHUNK)], 1
+            [winds[batch].at[chunk * CHUNK + inner].reshape(lines, LANES)[...] for inner in range(CHUNK)], 1
         )
 
     def prepare(step, carry):
@@ -165,6 +174,7 @@
         for inner in range(5):
             tile = step * 5 + inner
             wind_copy(1, tile).start()
+            wind_copy(2, tile).start()
             cos_a = coarse_cos[pl.ds(tile, 1), :]
             sin_a = coarse_sin[pl.ds(tile, 1), :]
             values = stack([cos_a * cos_b - sin_a * sin_b, -(sin_a * cos_b + cos_a * sin_b)], 1)
@@ -176,32 +186,36 @@
             waves_table[pl.ds(pl.multiple_of(second, LANES), LANES), :] = low
         return carry
 
-    def transform(f):
+    def transform(batch):
+        here_rows = slice(0, 16 * BATCHES[batch][2])
+
         def step(chunk, carry):
-            part = wind_chunk(f, chunk)
+            part = wind_chunk(batch, chunk)
             depth = 2 * CHUNK * LANES
             here = pl.ds(pl.multiple_of(chunk * depth, depth), depth)
-            total[...] += jnp.dot(
+            total[here_rows, :] += jnp.dot(
                 stack([part, part], 1), waves_table[here, :], preferred_element_type=F32
             )
             return carry
 
-        total[...] = jnp.zeros_like(total)
+        total[here_rows, :] = jnp.zeros((16 * BATCHES[batch][2], 2 * ENTRIES), F32)
         lax.fori_loop(0, STEPS, step, 0)
 
-    def publish(f):
+    def publish(batch):
+        rows = BATCHES[batch][2]
+        lines = 16 * rows
         for tile in range(4):
-            split[tile, :160] = total[:, LANES * tile : LANES * tile + LANES]
-        north = stack([split[tile, pl.ds(0, 80, stride=2), :] for tile in range(4)], 1)
-        south = stack([split[tile, pl.ds(1, 80, stride=2), :] for tile in range(4)], 1)
+            split[tile, :lines] = total[:lines, LANES * tile : LANES * tile + LANES]
+        north = stack([split[tile, pl.ds(0, 8 * rows, stride=2), :] for tile in range(4)], 1)
+        south = stack([split[tile, pl.ds(1, 8 * rows, stride=2), :] for tile in range(4)], 1)
         even = (north + south).astype(BF16)
         odd = (north - south).astype(BF16)
         paired = stack([even[:, :ENTRIES], odd[:, :ENTRIES], even[:, ENTRIES:], odd[:, ENTRIES:]], 0)
-        ordered = jnp.dot(row_order(), paired, preferred_element_type=F32).astype(BF16)
+        ordered = jnp.dot(row_order(rows), paired, preferred_element_type=F32).astype(BF16)
         blocks = stack(
             [
                 ordered[32 * line : 32 * line + 32] * rank_masks[slot]
-                for line in range(ROWS)
+                for line in range(rows)
                 for slot in range(4)
             ],
             0,
@@ -212,37 +226,35 @@
                 stack(
                     [placed[16 * g : 16 * g + 16, LANES * line : LANES * line + LANES] for g in range(8)], 1
                 )
-                for line in range(ROWS)
+                for line in range(rows)
             ],
             0,
         )
-        result = jnp.dot(group_order(), stacked, preferred_element_type=F32).astype(BF16)
-        flat = outgoing.at[f].reshape(HALF, LANES)
+        result = jnp.dot(group_order(rows), stacked, preferred_element_type=F32).astype(BF16)
+        flat = outgoing[batch].reshape(LANES * rows, LANES)
         for g in range(8):
-            flat[160 * g : 160 * g + 160, :] = result[:, LANES * g : LANES * g + LANES]
-
-    def own_copy(f):
-        return pltpu.make_async_copy(
-            outgoing.at[f, me], data.at[f, plane, inside], in_sems.at[f, 15]
-        )
-
-    def send_all(f):
-        own_copy(f).start()
+            flat[lines * g : lines * g + lines, :] = result[:, LANES * g : LANES * g + LANES]
+
+    def send_all(batch):
+        f, first, rows = BATCHES[batch]
+        place = data.at[f, plane, inside, pl.ds(first // 2, rows // 2)]
+        pltpu.make_async_copy(outgoing[batch].at[me], place, in_sems.at[batch, 15]).start()
 
         def send(target, index):
             pltpu.make_async_remote_copy(
-                src_ref=outgoing.at[f, target], dst_ref=data.at[f, plane, inside],
-                send_sem=out_sems.at[f], recv_sem=in_sems.at[f, index],
+                src_ref=outgoing[batch].at[target], dst_ref=place,
+                send_sem=out_sems.at[batch], recv_sem=in_sems.at[batch, index],
                 device_id=(target, core), device_id_type=MESH,
             ).start()
 
         everyone(send)
 
-    def arrive(f):
+    def arrive(batch):
+        f, first, rows = BATCHES[batch]
         for step in range(16):
             source = (row + 4 - FAR_LINES[step // 4]) % 4 * 4 + (column + 4 - FAR_LINES[step % 4]) % 4
-            part = data.at[f, :, source]
-            pltpu.make_async_copy(part, part, in_sems.at[f, step]).wait()
+            part = data.at[f, :, source, pl.ds(first // 2, rows // 2)]
+            pltpu.make_async_copy(part, part, in_sems.at[batch, step]).wait()
 
     unit = one_hot(iota((LANES, LANES), 0) == iota((LANES, LANES), 1))
 
@@ -254,19 +266,23 @@
     def project(turned, slot):
         return jnp.dot(turned[32 * slot : 32 * slot + 32], table[slot], preferred_element_type=F32)
 
-    lax.fori_loop(0, 8, prepare, 0)
+    lax.fori_loop(0, 4, prepare, 0)
     pl.semaphore_wait(barrier, 23)
     greet_plane(meet)
+    lax.fori_loop(4, 8, prepare, 0)
     transform(0)
     publish(0)
     pl.semaphore_wait(meet, 15)
     send_all(0)
-    for slot in range(4):
-        table_copy(slot).start()
-
     transform(1)
     publish(1)
     send_all(1)
+    for slot in range(4):
+        table_copy(slot).start()
+
+    transform(2)
+    publish(2)
+    send_all(2)
     for slot in range(4):
         table_share(slot).start()
 
@@ -317,6 +333,7 @@
     summed[...] = jnp.zeros_like(summed)
 
     arrive(0)
+    arrive(1)
     turned = turn(0)
     for slot in range(4):
         table_ready(slot)
@@ -333,7 +350,7 @@
             device_id=(me, other), device_id_type=MESH,
         )
 
-    arrive(1)
+    arrive(2)
     turned = turn(1)
     for slot in range(4):
         wave, last = waves[slot]
@@ -385,9 +402,9 @@
         device_id=(me, other), device_id_type=MESH,
     )
     swap.start()
-    for f in range(2):
-        sent = outgoing.at[f, pl.ds(0, 127)]
-        pltpu.make_async_copy(sent, sent, out_sems.at[f]).wait()
+    for batch in range(3):
+        sent = outgoing[batch].at[pl.ds(0, 127)]
+        pltpu.make_async_copy(sent, sent, out_sems.at[batch]).wait()
     for slot in range(4):
         table_share(slot).wait_send()
         hand_over(slot).wait_send()
@@ -406,7 +423,7 @@
 
 def tiles(wind):
     split = wind.transpose(0, 2, 1, 3).reshape(8, ROWS, 2, COARSE, LANES)
-    return split.transpose(0, 1, 3, 2, 4).reshape(80, COARSE, 2, LANES)
+    return split.transpose(0, 1, 3, 2, 4)
 
 
 def local(wind_u, wind_v, window_m, owner, legendre):
@@ -419,7 +436,7 @@
         in_specs=[hbm, hbm, vmem, vmem, hbm],
         out_specs=(vmem, vmem),
         scratch_shapes=[
-            pltpu.VMEM((2, COARSE, 80, 2, LANES), BF16),
+            *[pltpu.VMEM((COARSE, 8, rows, 2, LANES), BF16) for _, _, rows in BATCHES],
             pltpu.VMEM((COARSE, ENTRIES), F32),
             pltpu.VMEM((COARSE, ENTRIES), F32),
             pltpu.VMEM((LANES, ENTRIES), F32),
@@ -427,7 +444,7 @@
             pltpu.VMEM((2 * NLON, 2 * ENTRIES), BF16),
             pltpu.VMEM((160, 2 * ENTRIES), F32),
             pltpu.VMEM((4, 192, LANES), F32),
-            pltpu.VMEM((2, 128, 5, 2, LANES), BF16),
+            *[pltpu.VMEM((128, rows // 2, 2, LANES), BF16) for _, _, rows in BATCHES],
             pltpu.VMEM((2, 8, 16, 5, 2, LANES), BF16),
             pltpu.VMEM((4, HALF, HALF), BF16),
             pltpu.VMEM((4, 3, 8, HALF), F32),
@@ -439,8 +456,8 @@
             pltpu.VMEM((LANES, 2, LANES), F32),
             pltpu.VMEM((LANES, 2, LANES), F32),
             pltpu.VMEM((2, 2, LANES), F32),
-            dma((2, STEPS)), dma((4,)), dma((4,)), dma((4,)), pltpu.SemaphoreType.REGULAR,
-            dma((2,)), dma((2, 16)), dma((4,)), dma((4,)), dma((2,)), dma((2,)),
+            dma((3, STEPS)), dma((4,)), dma((4,)), dma((4,)), pltpu.SemaphoreType.REGULAR,
+            dma((3,)), dma((3, 16)), dma((4,)), dma((4,)), dma((2,)), dma((2,)),
         ],
         compiler_params=pltpu.CompilerParams(
             collective_id=0, has_side_effects=True, vmem_limit_bytes=VMEM_BYTES

time: 49.1 us -> 52 us (1.059)
  Pallas kernels: 46.9 us -> 49.9 us
    pallas_call x1, Pallas kernels: 46.9 us -> 49.9 us  [local(): pl.pallas_call(kernel, out_shape=(pltpu.VMEM((4, 2, 16, 2, COLS), F32), p...]
where the time goes in v8:
time: 52 us; the launch traced here: 51.9 us
  Pallas kernels  49.9 us (96%)
  local copies, waits for them, and re-layouts  1.43 us (3%)
  between operations  0.64 us (1%)
    pallas_call x1, Pallas kernels, local(): pl.pallas_call(kernel, out_shape=(pltpu.VMEM((4, 2, 16, 2, COLS), F32), p...  49.9 us
    unnamed x2, local copies, waits for them, and re-layouts  1.43 us

profile of v8, /device:TPU:1, one launch (start us, length us, event | category | flops | bytes accessed | tf_op | source)
XLA Modules:
  0.0 51.9 jit_solution(10933340488128694434)
XLA Ops:
  0.6 49.9 %shard_map.68 = (f32[4,2,16,2,640]{4,3,2,1,0:T(2,128)S(1)}, f32[5,2,16]{2,1,0:T(2,128)S(1)}) custom-call(bf16[8,10,40,2,128]{4,3,2,1,0:T(2,128)(2,1)} %bitcast.14, bf16[8,10,40,2,128]{4,3,2,1,0:T(2,128)(2,1)} %bitcast.15, s32[1,256]{1,0:T(1,128)} %bitcast.16, s32[1,256]{1,0:T(1,128)} %bitcast.17, bf16[4,1280,640]{2,1,0:T(8,128)(2,1)} %table_hbm.1), custom_call_target="tpu_custom_call" | custom-call | tf_op jit(solution)/shard_map/pallas_call | solution.py:433
  50.5 0.8 %copy.9 = f32[4,2,16,2,640]{4,3,2,1,0:T(2,128)} copy(f32[4,2,16,2,640]{4,3,2,1,0:T(2,128)S(1)} %get-tuple-element.6) | data formatting | bytes 1310720
  51.3 0.6 %copy.10 = f32[2,16,5]{1,0,2:T(2,128)} copy(f32[2,16,5]{1,0,2:T(2,128)S(1)} %bitcast.13) | data formatting | bytes 1280

commit v9 on v6

--- a/solution.py
+++ b/solution.py
@@ -20,7 +20,7 @@
 ROWS = 10
 HALF = 1280
 COLS = 640
-CHUNK = 20
+CHUNK = 40
 STEPS = COARSE // CHUNK
 
 NT = (((1,), (1,)), ((), ()))
@@ -276,6 +276,8 @@
         (iota((HALF, 2 * LANES), 0) % 10 == fold_lane % LANES // 64 * 5 + fold_turn) & (fold_turn < 5)
     )
     fold_rows[...] = one_hot(iota((LANES, HALF), 1) // 10 == iota((LANES, HALF), 0))
+    pair_row = iota((2 * LANES, 2 * LANES), 0)
+    interleave = one_hot(pair_row % 2 * LANES + pair_row // 2 == iota((2 * LANES, 2 * LANES), 1))
     spread_row = iota((16, 2 * LANES), 0)
     spread_lane = iota((16, 2 * LANES), 1)
     spread = one_hot((spread_row % 2 == spread_lane // LANES) & (spread_row // 2 == spread_lane % 8))
@@ -360,8 +362,11 @@
     upright = jnp.transpose(summed[...], (1, 0)).astype(BF16)
     placed = jnp.dot(upright, spread, preferred_element_type=F32).astype(BF16) * fold_mask[...]
     messages = jnp.dot(fold_rows[...], placed, preferred_element_type=F32)
-    for half in range(2):
-        fold_out[:, half, :] = messages[:, LANES * half : LANES * half + LANES]
+    messages = messages.astype(BF16)
+    messages = stack([messages[:, :LANES], messages[:, LANES:]], 0)
+    fold_out.reshape(2 * LANES, LANES)[...] = jnp.dot(
+        interleave, messages, preferred_element_type=F32
+    ).astype(BF16)
     fold_in[me] = fold_out[me]
 
     def send_fold(target, index):
@@ -374,10 +379,10 @@
     everyone(send_fold)
     arrived = fold_in.at[pl.ds(0, 127)]
     pltpu.make_async_copy(arrived, arrived, fold_sems.at[1]).wait()
-    lines = fold_in.reshape(2 * LANES, LANES)
-    folded = lines[0:8, :]
+    lines = fold_in.reshape(2 * LANES, LANES)[...].astype(F32)
+    folded = lines[0:8]
     for index in range(1, 32):
-        folded = folded + lines[8 * index : 8 * index + 8, :]
+        folded = folded + lines[8 * index : 8 * index + 8]
     final[core] = folded[0:2] + folded[2:4] + folded[4:6] + folded[6:8]
     swap = pltpu.make_async_remote_copy(
         src_ref=final.at[core], dst_ref=final.at[core],
@@ -436,8 +441,8 @@
             pltpu.VMEM((4, 2, 8, 2, COLS), F32),
             pltpu.VMEM((HALF, 2 * LANES), BF16),
             pltpu.VMEM((LANES, HALF), BF16),
-            pltpu.VMEM((LANES, 2, LANES), F32),
-            pltpu.VMEM((LANES, 2, LANES), F32),
+            pltpu.VMEM((LANES, 2, LANES), BF16),
+            pltpu.VMEM((LANES, 2, LANES), BF16),
             pltpu.VMEM((2, 2, LANES), F32),
             dma((2, STEPS)), dma((4,)), dma((4,)), dma((4,)), pltpu.SemaphoreType.REGULAR,
             dma((2,)), dma((2, 16)), dma((4,)), dma((4,)), dma((2,)), dma((2,)),

time: 49.1 us -> 48.7 us (level)
  no operation moved by 1% of the time
where the time goes in v9:
time: 48.7 us; the launch traced here: 48.6 us
  Pallas kernels  46.6 us (96%)
  local copies, waits for them, and re-layouts  1.43 us (3%)
  between operations  0.64 us (1%)
    pallas_call x1, Pallas kernels, local(): pl.pallas_call(kernel, out_shape=(pltpu.VMEM((4, 2, 16, 2, COLS), F32), p...  46.6 us
    unnamed x2, local copies, waits for them, and re-layouts  1.43 us

profile of v9, /device:TPU:1, one launch (start us, length us, event | category | flops | bytes accessed | tf_op | source)
XLA Modules:
  0.0 48.6 jit_solution(11847539728059361530)
XLA Ops:
  0.6 46.6 %shard_map.68 = (f32[4,2,16,2,640]{4,3,2,1,0:T(2,128)S(1)}, f32[5,2,16]{2,1,0:T(2,128)S(1)}) custom-call(bf16[80,40,2,128]{3,2,1,0:T(2,128)(2,1)} %bitcast.18, bf16[80,40,2,128]{3,2,1,0:T(2,128)(2,1)} %bitcast.19, s32[1,256]{1,0:T(1,128)} %bitcast.20, s32[1,256]{1,0:T(1,128)} %bitcast.21, bf16[4,1280,640]{2,1,0:T(8,128)(2,1)} %table_hbm.1), custom_call_target="tpu_custom_call" | custom-call | tf_op jit(solution)/shard_map/pallas_call | solution.py:421
  47.2 0.8 %copy.11 = f32[4,2,16,2,640]{4,3,2,1,0:T(2,128)} copy(f32[4,2,16,2,640]{4,3,2,1,0:T(2,128)S(1)} %get-tuple-element.6) | data formatting | bytes 1310720
  48.0 0.6 %copy.12 = f32[2,16,5]{1,0,2:T(2,128)} copy(f32[2,16,5]{1,0,2:T(2,128)S(1)} %bitcast.17) | data formatting | bytes 1280
